TPU v7x, 32 devices: a whole 2x2x4 slice. The times are simulated.
32 devices in a mesh: groups: 2 (over x), space: 16 (over z, y, core).
Axes of the slice: x: 2, y: 2, z: 4, core: 2. Of those that a mesh axis runs over, the one named last changes fastest.
Arguments:
- grid_latent: bfloat16 [65536, 512], P(('groups', 'space')), parts along dimension 0, may hold values from -6 to 6
- mesh_latent: bfloat16 [8192, 512], P(('groups', 'space')), parts along dimension 0, may hold values from -6 to 6
- out_cotangent: bfloat16 [8192, 512], P(('groups', 'space')), parts along dimension 0, may hold values from -6 to 6
- matrices: bfloat16 [2, 4, 512, 512], replicated, may hold values from -0.25 to 0.25
- norm_gains: float32 [2, 512], replicated, may hold values from 0.5 to 1.5
- edge_embeddings: float32 [2, 4, 512], replicated, may hold values from -3 to 3
- enc_attributes: float32 [4, 32768], P(None, 'space'), may hold values from -6 to 6
- proc_attributes: float32 [4, 32768], P(None, 'space'), may hold values from -6 to 6
- enc_send_block: int32 [256], P('space'), may hold values from 0 to 39, as said below
- enc_recv_block: int32 [256], P('space'), may hold values from 0 to 3, as said below
- enc_send_slot: int32 [256, 128], P('space'), may hold values from 0 to 63
- enc_recv_slot: int32 [256, 128], P('space'), may hold values from 0 to 63
- enc_count: int32 [16], P('space'), may hold values from 4 to 16, as said below
- proc_send_block: int32 [256], P('space'), may hold values from 0 to 5, as said below
- proc_recv_block: int32 [256], P('space'), may hold values from 0 to 3, as said below
- proc_send_slot: int32 [256, 128], P('space'), may hold values from 0 to 63
- proc_recv_slot: int32 [256, 128], P('space'), may hold values from 0 to 63
- proc_count: int32 [16], P('space'), may hold values from 4 to 16, as said below
Outputs:
- mesh_out: bfloat16 [8192, 512], P(('groups', 'space')), parts along dimension 0
- grid_grad: bfloat16 [65536, 512], P(('groups', 'space')), parts along dimension 0
- mesh_grad: bfloat16 [8192, 512], P(('groups', 'space')), parts along dimension 0
- matrix_grads: float32 [4, 4, 512, 512], P('groups', None, None, 'space'), parts along dimension 0
- gain_grads: float32 [4, 512], P('groups', 'space'), parts along dimension 0
- embedding_grads: float32 [4, 4, 512], P('groups', None, 'space'), parts along dimension 0
There are 2 independent parts, one for each index of `groups`. A program takes and returns all parts, laid end to end along the dimension named above; an argument that names none is the same for every part. Nothing has to cross between parts.
Inputs may be any that keep to these rules, and one draw needn't show every extreme that they name: `enc_send_block`: counts blocks of 64 of the slab's extended grid rows; the first slab names none before its own rows and the last none after them. `enc_recv_block`: counts blocks of 64 of the slab's own mesh rows. `enc_count`: a multiple of 4; the live blocks come first in the slab's list. `proc_send_block`: counts blocks of 64 of the slab's extended mesh rows; the first slab names none before its own rows and the last none after them. `proc_recv_block`: counts blocks of 64 of the slab's own mesh rows. `proc_count`: a multiple of 4; the live blocks come first in the slab's list.
All inputs are finite; a program needn't handle non-finite values.
Results may differ from a plain program's by a relative error of at most 0.017.
Values may be sent and summed in bfloat16 or wider, within the bound.
A program may use at most 192 MiB of HBM per device.

v0:
```python
import functools

import jax
import jax.numpy as jnp
from jax import lax
from jax.experimental import pallas as pl
from jax.experimental.pallas import tpu as pltpu
from jax.sharding import PartitionSpec as P

BLK = 64
EPB = 128
HG = 256
HM = 64
GB = 4
GE = GB * EPB
EPS = 1e-05
SMALL = 128
VMEM_LIMIT = 56 * 1024 * 1024

f32 = jnp.float32
bf16 = jnp.bfloat16


def dot(a, b):
    return jnp.dot(a, b, preferred_element_type=f32)


def dot_tb(a, b):
    return lax.dot_general(a, b, (((1,), (1,)), ((), ())), preferred_element_type=f32)


def dot_ta(a, b):
    return lax.dot_general(a, b, (((0,), (0,)), ((), ())), preferred_element_type=f32)


def one_hot_pull(columns, group, base, width):
    lanes = lax.broadcasted_iota(jnp.int32, (EPB, width), 1)
    parts = []
    for m in range(GB):
        b = group * GB + m
        parts.append((lanes == columns[:, b : b + 1] + base[m]).astype(f32).astype(bf16))
    return jnp.concatenate(parts, axis=0)


def one_hot_push(slots_ref, group, base, width):
    rows = lax.broadcasted_iota(jnp.int32, (width, EPB), 0)
    parts = []
    for m in range(GB):
        b = group * GB + m
        parts.append((rows == slots_ref[b : b + 1, :] + base[m]).astype(f32).astype(bf16))
    return jnp.concatenate(parts, axis=1)


SEND_BASE = [m * BLK for m in range(GB)]


def recv_base(recv_block, group):
    return [recv_block[group * GB + m] * BLK for m in range(GB)]


def edges_forward(group, send_tiles, recv_proj, cols_s, cols_r, recv_slot, recv_block, attr, emb):
    base = recv_base(recv_block, group)
    width = recv_proj.shape[0]
    pre = dot(one_hot_pull(cols_s, group, SEND_BASE, GB * BLK), send_tiles)
    pre = pre + dot(one_hot_pull(cols_r, group, base, width), recv_proj)
    pre = pre + dot_ta(attr[:, group * GE : (group + 1) * GE], emb)
    gate = 0.5 * jnp.tanh(0.5 * pre) + 0.5
    act = pre * gate
    slope = gate + act * (1.0 - gate)
    summed = dot(one_hot_push(recv_slot, group, base, width), act.astype(bf16))
    return summed, slope.astype(bf16)


def edges_backward(group, d_agg, slope, cols_r, send_slot, recv_slot, recv_block, attr):
    base = recv_base(recv_block, group)
    width = d_agg.shape[0]
    d_pre = dot(one_hot_pull(cols_r, group, base, width), d_agg) * slope.astype(f32)
    d_pre = d_pre.astype(bf16)
    d_send = dot(one_hot_push(send_slot, group, SEND_BASE, GB * BLK), d_pre)
    d_recv = dot(one_hot_push(recv_slot, group, base, width), d_pre)
    d_emb = dot(attr[:, group * GE : (group + 1) * GE], d_pre)
    return d_send, d_recv, d_emb


def tail_forward(mixed, latent, gain):
    u = mixed * (0.5 * jnp.tanh(0.5 * mixed) + 0.5)
    c = u - jnp.mean(u, axis=-1, keepdims=True)
    v = jnp.mean(c * c, axis=-1, keepdims=True)
    return (latent.astype(f32) + c * lax.rsqrt(v + EPS) * gain).astype(bf16)


def tail_backward(mixed, cot, gain):
    s = 0.5 * jnp.tanh(0.5 * mixed) + 0.5
    u = mixed * s
    c = u - jnp.mean(u, axis=-1, keepdims=True)
    r = lax.rsqrt(jnp.mean(c * c, axis=-1, keepdims=True) + EPS)
    n = c * r
    d_gain = jnp.sum(cot * n, axis=0, keepdims=True)
    dn = cot * gain
    du = r * (dn - jnp.mean(dn, axis=-1, keepdims=True) - n * jnp.mean(dn * n, axis=-1, keepdims=True))
    return (du * (s + u * (1.0 - s))).astype(bf16), d_gain


def write_small(w_ref, d_emb, d_gain):
    width = d_emb.shape[1]
    pad = jnp.zeros((SMALL - 16 - 8, width), f32)
    block = jnp.concatenate([d_emb, jnp.broadcast_to(d_gain, (8, width)), pad], axis=0)
    w_ref[:, 4 * width :] = block.T.astype(bf16)


def enc_forward_kernel(
    send_block, recv_block, count, own, lo, hi, latent, w, gains, emb, attr, send_slot, recv_slot,
    out, agg_out, mixed_out, slope_out, tiles_out, ext, acc, sems,
):
    rows = own.shape[0]
    copies = [
        pltpu.make_async_copy(own, ext.at[pl.ds(HG, rows)], sems.at[0]),
        pltpu.make_async_copy(lo, ext.at[pl.ds(0, HG)], sems.at[1]),
        pltpu.make_async_copy(hi, ext.at[pl.ds(HG + rows, HG)], sems.at[2]),
    ]
    for c in copies:
        c.start()
    recv_proj = dot(latent[...], w[0, 1]).astype(bf16)
    cols_s = send_slot[...].T
    cols_r = recv_slot[...].T
    acc[...] = jnp.zeros_like(acc)
    for c in copies:
        c.wait()
    for group in range(send_slot.shape[0] // GB):

        @pl.when(group * GB < count[0])
        def _(group=group):
            for m in range(GB):
                at = group * GB + m
                start = pl.multiple_of(send_block[at] * BLK, BLK)
                tiles_out[at * BLK : (at + 1) * BLK, :] = ext[pl.ds(start, BLK), :]
            tiles = tiles_out[group * GB * BLK : (group + 1) * GB * BLK, :]
            send_proj = dot(tiles, w[0, 0]).astype(bf16)
            summed, slope = edges_forward(
                group, send_proj, recv_proj, cols_s, cols_r, recv_slot, recv_block, attr, emb[0]
            )
            slope_out[group * GE : (group + 1) * GE, :] = slope
            acc[...] += summed

    agg = acc[...].astype(bf16)
    agg_out[...] = agg
    mixed = dot(latent[...], w[0, 2]) + dot(agg, w[0, 3])
    mixed_out[...] = mixed
    out[...] = tail_forward(mixed, latent[...], gains[0:1, :])


def proc_kernel(
    send_block, recv_block, count, enc_out, lo, hi, cot, w, gains, emb, attr, send_slot, recv_slot,
    out, d_latent, rim_lo, rim_hi, w_out, ext, proj, slopes, acc, d_send_acc, d_emb_acc,
):
    rows, width = enc_out.shape
    groups = send_slot.shape[0] // GB
    latent = enc_out[...]
    ext[0:HM, :] = lo[...]
    ext[HM : HM + rows, :] = latent
    ext[HM + rows :, :] = hi[...]
    proj[...] = dot(ext[...], w[0, 0]).astype(bf16)
    recv_proj = dot(latent, w[0, 1]).astype(bf16)
    cols_s = send_slot[...].T
    cols_r = recv_slot[...].T
    acc[...] = jnp.zeros_like(acc)
    for group in range(groups):

        @pl.when(group * GB < count[0])
        def _(group=group):
            tiles = [
                proj[pl.ds(pl.multiple_of(send_block[group * GB + m] * BLK, BLK), BLK), :]
                for m in range(GB)
            ]
            summed, slope = edges_forward(
                group, jnp.concatenate(tiles, axis=0), recv_proj, cols_s, cols_r, recv_slot,
                recv_block, attr, emb[0],
            )
            slopes[group * GE : (group + 1) * GE, :] = slope
            acc[...] += summed

    agg = acc[...].astype(bf16)
    mixed = dot(latent, w[0, 2]) + dot(agg, w[0, 3])
    out[...] = tail_forward(mixed, latent, gains[1:2, :])

    cot32 = cot[...].astype(f32)
    g, d_gain = tail_backward(mixed, cot32, gains[1:2, :])
    d_agg = dot_tb(g, w[0, 3]).astype(bf16)
    acc[...] = jnp.zeros_like(acc)
    d_send_acc[...] = jnp.zeros_like(d_send_acc)
    d_emb_acc[...] = jnp.zeros_like(d_emb_acc)
    for group in range(groups):

        @pl.when(group * GB < count[0])
        def _(group=group):
            d_send, d_recv, d_emb = edges_backward(
                group, d_agg, slopes[group * GE : (group + 1) * GE, :], cols_r, send_slot,
                recv_slot, recv_block, attr,
            )
            for m in range(GB):
                start = pl.multiple_of(send_block[group * GB + m] * BLK, BLK)
                d_send_acc[pl.ds(start, BLK), :] += d_send[m * BLK : (m + 1) * BLK, :]
            acc[...] += d_recv
            d_emb_acc[...] += d_emb

    d_send = d_send_acc[...].astype(bf16)
    d_recv = acc[...].astype(bf16)
    d_rows = dot_tb(d_send, w[0, 0])
    rim_lo[...] = d_rows[0:HM, :].astype(bf16)
    rim_hi[...] = d_rows[HM + rows :, :].astype(bf16)
    d_latent[...] = (
        cot32 + dot_tb(g, w[0, 2]) + dot_tb(d_recv, w[0, 1]) + d_rows[HM : HM + rows, :]
    )
    w_out[:, 0:width] = dot_ta(d_send, ext[...]).astype(bf16)
    w_out[:, width : 2 * width] = dot_ta(d_recv, latent).astype(bf16)
    w_out[:, 2 * width : 3 * width] = dot_ta(g, latent).astype(bf16)
    w_out[:, 3 * width : 4 * width] = dot_ta(g, agg).astype(bf16)
    write_small(w_out, d_emb_acc[...], d_gain)


def enc_backward_kernel(
    send_block, recv_block, count, d_latent, back_lo, back_hi, latent, agg, mixed, slopes, tiles,
    w, gains, attr, send_slot, recv_slot,
    mesh_grad, grid_own, grid_lo, grid_hi, w_out, grid_acc, acc, d_emb_acc, w0_acc, cot_ref,
):
    rows, width = latent.shape
    groups = send_slot.shape[0] // GB
    cot_ref[...] = d_latent[...]
    cot_ref[0:HM, :] += back_lo[...].astype(f32)
    cot_ref[rows - HM :, :] += back_hi[...].astype(f32)
    cot = cot_ref[...].astype(bf16).astype(f32)
    g, d_gain = tail_backward(mixed[...], cot, gains[0:1, :])
    d_agg = dot_tb(g, w[0, 3]).astype(bf16)
    cols_r = recv_slot[...].T
    grid_acc[...] = jnp.zeros_like(grid_acc)
    acc[...] = jnp.zeros_like(acc)
    d_emb_acc[...] = jnp.zeros_like(d_emb_acc)
    w0_acc[...] = jnp.zeros_like(w0_acc)
    for group in range(groups):

        @pl.when(group * GB < count[0])
        def _(group=group):
            d_send, d_recv, d_emb = edges_backward(
                group, d_agg, slopes[group * GE : (group + 1) * GE, :], cols_r, send_slot,
                recv_slot, recv_block, attr,
            )
            d_send = d_send.astype(bf16)
            d_rows = dot_tb(d_send, w[0, 0])
            for m in range(GB):
                start = pl.multiple_of(send_block[group * GB + m] * BLK, BLK)
                grid_acc[pl.ds(start, BLK), :] += d_rows[m * BLK : (m + 1) * BLK, :]
            acc[...] += d_recv
            d_emb_acc[...] += d_emb
            w0_acc[...] += dot_ta(d_send, tiles[group * GB * BLK : (group + 1) * GB * BLK, :])

    own = grid_own.shape[0]
    grid_lo[...] = grid_acc[0:HG, :].astype(bf16)
    grid_hi[...] = grid_acc[HG + own :, :].astype(bf16)
    grid_own[...] = grid_acc[HG : HG + own, :].astype(bf16)
    d_recv = acc[...].astype(bf16)
    mesh_grad[...] = (cot + dot_tb(g, w[0, 2]) + dot_tb(d_recv, w[0, 1])).astype(bf16)
    w_out[:, 0:width] = w0_acc[...].astype(bf16)
    w_out[:, width : 2 * width] = dot_ta(d_recv, latent[...]).astype(bf16)
    w_out[:, 2 * width : 3 * width] = dot_ta(g, latent[...]).astype(bf16)
    w_out[:, 3 * width : 4 * width] = dot_ta(g, agg[...]).astype(bf16)
    write_small(w_out, d_emb_acc[...], d_gain)


smem = pl.BlockSpec(memory_space=pltpu.SMEM)
hbm = pl.BlockSpec(memory_space=pl.ANY)
vmem = pl.BlockSpec(memory_space=pltpu.VMEM)


def layer_spec(layer, shape):
    tail = (0,) * (len(shape) - 1)
    return pl.BlockSpec((1,) + shape[1:], lambda i: (layer,) + tail)


def call(kernel, in_specs, out_shape, scratch, flops):
    return pl.pallas_call(
        kernel,
        grid=(1,),
        in_specs=in_specs,
        out_specs=[vmem] * len(out_shape),
        out_shape=out_shape,
        scratch_shapes=scratch,
        compiler_params=pltpu.CompilerParams(vmem_limit_bytes=VMEM_LIMIT),
        cost_estimate=pl.CostEstimate(flops=flops, bytes_accessed=10_000_000, transcendentals=0),
    )


def shift(up, down, axis):
    ends = lax.axis_size(axis) - 1
    return (
        lax.ppermute(up, axis, [(i, i + 1) for i in range(ends)]),
        lax.ppermute(down, axis, [(i + 1, i) for i in range(ends)]),
    )


def split_rows(a, axis, order):
    top = lax.reduce_precision(a, 8, 7)
    rest = a - top
    pieces = [top if k else rest for k in order]
    return jnp.concatenate(pieces + [jnp.zeros_like(a)], axis=axis).astype(bf16)


def per_device(
    grid_latent, mesh_latent, out_cotangent, matrices, norm_gains, edge_embeddings,
    enc_attributes, proc_attributes, enc_send_block, enc_recv_block, enc_send_slot,
    enc_recv_slot, enc_count, proc_send_block, proc_recv_block, proc_send_slot,
    proc_recv_slot, proc_count,
):
    rows, width = mesh_latent.shape
    own = grid_latent.shape[0]
    blocks = enc_send_block.shape[0]
    p_blocks = proc_send_block.shape[0]
    sds = jax.ShapeDtypeStruct
    emb = split_rows(edge_embeddings, 1, (1, 1, 0))
    enc_attr = split_rows(enc_attributes, 0, (1, 0, 1))
    proc_attr = split_rows(proc_attributes, 0, (1, 0, 1))

    lo, hi = shift(grid_latent[own - HG :], grid_latent[:HG], "space")
    enc_out, agg, mixed, slopes, tiles = call(
        enc_forward_kernel,
        [smem] * 3 + [hbm] * 3 + [vmem, layer_spec(0, matrices.shape), vmem, layer_spec(0, emb.shape), vmem, vmem, vmem],
        [
            sds((rows, width), bf16),
            sds((rows, width), bf16),
            sds((rows, width), f32),
            sds((blocks * EPB, width), bf16),
            sds((blocks * BLK, width), bf16),
        ],
        [
            pltpu.VMEM((own + 2 * HG, width), bf16),
            pltpu.VMEM((rows, width), f32),
            pltpu.SemaphoreType.DMA((3,)),
        ],
        4_000_000_000,
    )(
        enc_send_block, enc_recv_block, enc_count, grid_latent, lo, hi, mesh_latent, matrices,
        norm_gains, emb, enc_attr, enc_send_slot, enc_recv_slot,
    )

    lo, hi = shift(enc_out[rows - HM :], enc_out[:HM], "space")
    mesh_out, d_latent, rim_lo, rim_hi, proc_w = call(
        proc_kernel,
        [smem] * 3 + [vmem] * 4 + [layer_spec(1, matrices.shape), vmem, layer_spec(1, emb.shape), vmem, vmem, vmem],
        [
            sds((rows, width), bf16),
            sds((rows, width), f32),
            sds((HM, width), bf16),
            sds((HM, width), bf16),
            sds((width, 4 * width + SMALL), bf16),
        ],
        [
            pltpu.VMEM((rows + 2 * HM, width), bf16),
            pltpu.VMEM((rows + 2 * HM, width), bf16),
            pltpu.VMEM((p_blocks * EPB, width), bf16),
            pltpu.VMEM((rows, width), f32),
            pltpu.VMEM((rows + 2 * HM, width), f32),
            pltpu.VMEM((16, width), f32),
        ],
        8_000_000_000,
    )(
        proc_send_block, proc_recv_block, proc_count, enc_out, lo, hi, out_cotangent, matrices,
        norm_gains, emb, proc_attr, proc_send_slot, proc_recv_slot,
    )

    back_lo, back_hi = shift(rim_hi, rim_lo, "space")
    proc_sum = lax.psum_scatter(proc_w, "space", scatter_dimension=0, tiled=True)
    mesh_grad, grid_own, grid_lo, grid_hi, enc_w = call(
        enc_backward_kernel,
        [smem] * 3 + [vmem] * 8 + [layer_spec(0, matrices.shape), vmem, vmem, vmem, vmem],
        [
            sds((rows, width), bf16),
            sds((own, width), bf16),
            sds((HG, width), bf16),
            sds((HG, width), bf16),
            sds((width, 4 * width + SMALL), bf16),
        ],
        [
            pltpu.VMEM((own + 2 * HG, width), f32),
            pltpu.VMEM((rows, width), f32),
            pltpu.VMEM((16, width), f32),
            pltpu.VMEM((width, width), f32),
            pltpu.VMEM((rows, width), f32),
        ],
        8_000_000_000,
    )(
        enc_send_block, enc_recv_block, enc_count, d_latent, back_lo, back_hi, mesh_latent, agg,
        mixed, slopes, tiles, matrices, norm_gains, enc_attr, enc_send_slot, enc_recv_slot,
    )
    from_prev, from_next = shift(grid_hi, grid_lo, "space")
    grid_grad = grid_own.at[:HG].add(from_prev).at[own - HG :].add(from_next)
    enc_sum = lax.psum_scatter(enc_w, "space", scatter_dimension=0, tiled=True)

    sums = jnp.stack([enc_sum, proc_sum]).astype(f32)
    columns = sums.shape[1]
    matrix_grads = sums[:, :, : 4 * width].reshape(2, columns, 4, width).transpose(0, 2, 3, 1)
    small = sums[:, :, 4 * width :].transpose(0, 2, 1)
    embedding_grads = small[:, 0:4] + small[:, 4:8]
    gain_grads = small[:, 16]
    return (mesh_out, grid_grad, mesh_grad, matrix_grads, gain_grads, embedding_grads)


def solution(mesh):
    rows = P(("groups", "space"), None)
    lists = (P("space"), P("space"), P("space", None), P("space", None), P("space"))
    return jax.shard_map(
        per_device,
        mesh=mesh,
        in_specs=(rows, rows, rows, P(), P(), P(), P(None, "space"), P(None, "space")) + lists + lists,
        out_specs=(
            rows,
            rows,
            rows,
            P("groups", None, None, "space"),
            P("groups", "space"),
            P("groups", None, "space"),
        ),
        check_vma=False,
    )
```

profile of v0, /device:TPU:0, one launch (start us, length us, event | category | flops | bytes accessed | tf_op | source)
XLA Modules:
  0.0 191.7 jit_solution(1302623935623534016)
XLA Ops:
  7.2 1.1 fusion.4
  8.3 1.3 collective-permute-start.1
  9.6 3.0 %collective-permute-start = (bf16[256,512]{1,0:T(8,128)(2,1)S(1)}, bf16[256,512]{1,0:T(8,128)(2,1)S(1)}, u32[]{:S(2)}, u32[]{:S(2)}) collective-permute-start(bf16[256,512]{1,0:T(8,128)(2,1)S(1)} %get-tuple-element.73), channel_id=1, source_target_pairs={{0,1},{1,2},{2,3},{3,4},{4,5},{5,6},{6,7},{7,8},{8,9},{9,10},{10,1... | collective-permute-start | bytes 786440 | tf_op jit(solution)/shard_map/ppermute | solution.py:295
  12.7 0.8 fusion.1
  13.5 0.7 maximum_maximum_fusion.1
  14.3 0.7 reduce-precision_convert_fusion.2
  15.6 0.7 maximum_maximum_fusion.2.emb
  16.3 0.7 copy-done
  17.1 6.5 %shard_map.217 = (bf16[256,512]{1,0:T(8,128)(2,1)}, bf16[256,512]{1,0:T(8,128)(2,1)}, f32[256,512]{1,0:T(8,128)}, bf16[2048,512]{1,0:T(8,128)(2,1)}, bf16[1024,512]{1,0:T(8,128)(2,1)}) custom-call(s32[16]{0:T(128)} %send_block.5, s32[16]{0:T(128)} %recv_block.5, s32[1]{0:T(128)S(6)} %copy.33.count, bf16[2048,512]{1,0:T(8,128)(2,1)} %own.1, ...), custom_call_target="tpu_custom_call" | custom-call | flops 4000000000 | bytes 10000000 | tf_op jit(solution)/shard_map/pallas_call | solution.py:323
  23.6 0.9 fusion.5
  24.5 1.3 collective-permute-start.3
  25.8 6.4 %collective-permute-start.2 = (bf16[64,512]{1,0:T(8,128)(2,1)S(1)}, bf16[64,512]{1,0:T(8,128)(2,1)S(1)}, u32[]{:S(2)}, u32[]{:S(2)}) collective-permute-start(bf16[64,512]{1,0:T(8,128)(2,1)S(1)} %get-tuple-element.75), channel_id=1, source_target_pairs={{0,1},{1,2},{2,3},{3,4},{4,5},{5,6},{6,7},{7,8},{8,9},{9,10},{10,1... | collective-permute-start | bytes 196616 | tf_op jit(solution)/shard_map/ppermute | solution.py:295
  33.8 10.1 %shard_map.218 = (bf16[256,512]{1,0:T(8,128)(2,1)}, f32[256,512]{1,0:T(8,128)}, bf16[64,512]{1,0:T(8,128)(2,1)}, bf16[64,512]{1,0:T(8,128)(2,1)}, bf16[512,2176]{1,0:T(8,128)(2,1)}) custom-call(s32[16]{0:T(128)} %send_block.4, s32[16]{0:T(128)} %recv_block.4, s32[1]{0:T(128)S(6)} %copy.34.count, bf16[256,512]{1,0:T(8,128)(2,1)} %get-tuple-element.45.enc_out, ...), custom_call_target="tpu_custom_call" | custom-call | flops 8000000000 | bytes 10000000 | tf_op jit(solution)/shard_map/pallas_call | solution.py:345
  44.0 0.8 copy-done.5
  44.7 4.2 %collective-permute-start.4 = (bf16[64,512]{1,0:T(8,128)(2,1)S(1)}, bf16[64,512]{1,0:T(8,128)(2,1)S(1)}, u32[]{:S(2)}, u32[]{:S(2)}) collective-permute-start(bf16[64,512]{1,0:T(8,128)(2,1)S(1)} %copy-done.5), channel_id=1, source_target_pairs={{0,1},{1,2},{2,3},{3,4},{4,5},{5,6},{6,7},{7,8},{8,9},{9,10},{10,1... | collective-permute-start | bytes 196616 | tf_op jit(solution)/shard_map/ppermute | solution.py:295
  48.9 1.3 collective-permute-start.5
  50.2 3.7 %collective-permute-done.5.back_hi = bf16[64,512]{1,0:T(8,128)(2,1)S(1)} collective-permute-done((bf16[64,512]{1,0:T(8,128)(2,1)S(1)}, bf16[64,512]{1,0:T(8,128)(2,1)S(1)}, u32[]{:S(2)}, u32[]{:S(2)}) %collective-permute-start.5) | collective-permute-done | bytes 65568 | tf_op jit(solution)/shard_map/ppermute | solution.py:296
  53.9 0.6 copy-done.8
  54.5 8.7 %shard_map.219 = (bf16[256,512]{1,0:T(8,128)(2,1)}, bf16[2048,512]{1,0:T(8,128)(2,1)}, bf16[256,512]{1,0:T(8,128)(2,1)}, bf16[256,512]{1,0:T(8,128)(2,1)}, bf16[512,2176]{1,0:T(8,128)(2,1)}) custom-call(s32[16]{0:T(128)} %send_block.5, s32[16]{0:T(128)} %recv_block.5, s32[1]{0:T(128)S(6)} %copy.33.count, f32[256,512]{1,0:T(8,128)} %get-tuple-element.47.d_latent, ...), custom_call_target="tpu_custom_call" | custom-call | flops 8000000000 | bytes 10000000 | tf_op jit(solution)/shard_map/pallas_call | solution.py:371
  63.2 0.9 copy-done.3
  64.2 5.0 %collective-permute-start.6 = (bf16[256,512]{1,0:T(8,128)(2,1)S(1)}, bf16[256,512]{1,0:T(8,128)(2,1)S(1)}, u32[]{:S(2)}, u32[]{:S(2)}) collective-permute-start(bf16[256,512]{1,0:T(8,128)(2,1)S(1)} %copy-done.3), channel_id=1, source_target_pairs={{0,1},{1,2},{2,3},{3,4},{4,5},{5,6},{6,7},{7,8},{8,9},{9,10},{10,1... | collective-permute-start | bytes 786440 | tf_op jit(solution)/shard_map/ppermute | solution.py:295
  69.1 1.3 collective-permute-start.7
  70.4 1.7 add_dynamic-update-slice_fusion
  72.2 0.9 collective-permute-done.7
  73.1 1.7 fusion
  74.8 40.2 %reduce-scatter.5.cloned.1.call-done = bf16[32,2176]{1,0:T(8,128)(2,1)} async-done(((bf16[512,2176]{1,0:T(8,128)(2,1)}), bf16[32,2176]{1,0:T(8,128)(2,1)}) %reduce-scatter.5.cloned.1.call-update) | async-done | bytes 139280 | tf_op jit(solution)/shard_map/reduce_scatter | solution.py:370
  115.0 65.8 %reduce-scatter.3.cloned.1.call-done = bf16[32,2176]{1,0:T(8,128)(2,1)} async-done(((bf16[512,2176]{1,0:T(8,128)(2,1)}), bf16[32,2176]{1,0:T(8,128)(2,1)}) %reduce-scatter.3.cloned.1.call-update) | async-done | bytes 139280 | tf_op jit(solution)/shard_map/reduce_scatter | solution.py:395
  180.8 0.7 convert_bitcast_fusion
  181.5 0.7 slice_reduce_fusion
  182.3 1.0 maximum_convert_fusion
  183.3 0.7 copy.27
  184.0 0.8 copy.30
  (30 shorter events, 1.3 us)
Async XLA Ops:
  7.2 107.8 %reduce-scatter.5.cloned.1.call-start = ((), (), s32[]{:S(2)}) async-start(), calls=%async_computation.3 | async-start | bytes 2367488 | tf_op jit(solution)/shard_map/reduce_scatter | solution.py:370
  8.3 8.0 %collective-permute-start.1 = (bf16[256,512]{1,0:T(8,128)(2,1)S(1)}, bf16[256,512]{1,0:T(8,128)(2,1)S(1)}, u32[]{:S(2)}, u32[]{:S(2)}) collective-permute-start(bf16[256,512]{1,0:T(8,128)(2,1)S(1)} %get-tuple-element.72), channel_id=1, source_target_pairs={{1,0},{2,1},{3,2},{4,3},{5,4},{6,5},{7,6},{8,7},{9,8},{10,9},{11,1... | collective-permute-start | bytes 786440 | tf_op jit(solution)/shard_map/ppermute | solution.py:296
  9.6 6.7 %collective-permute-start = (bf16[256,512]{1,0:T(8,128)(2,1)S(1)}, bf16[256,512]{1,0:T(8,128)(2,1)S(1)}, u32[]{:S(2)}, u32[]{:S(2)}) collective-permute-start(bf16[256,512]{1,0:T(8,128)(2,1)S(1)} %get-tuple-element.73), channel_id=1, source_target_pairs={{0,1},{1,2},{2,3},{3,4},{4,5},{5,6},{6,7},{7,8},{8,9},{9,10},{10,1... | collective-permute-start | bytes 786440 | tf_op jit(solution)/shard_map/ppermute | solution.py:295
  16.3 0.7 copy-start
  16.3 0.8 copy-start.1
  24.5 8.4 %collective-permute-start.3 = (bf16[64,512]{1,0:T(8,128)(2,1)S(1)}, bf16[64,512]{1,0:T(8,128)(2,1)S(1)}, u32[]{:S(2)}, u32[]{:S(2)}) collective-permute-start(bf16[64,512]{1,0:T(8,128)(2,1)S(1)} %get-tuple-element.74), channel_id=1, source_target_pairs={{1,0},{2,1},{3,2},{4,3},{5,4},{6,5},{7,6},{8,7},{9,8},{10,9},{11,1... | collective-permute-start | bytes 196616 | tf_op jit(solution)/shard_map/ppermute | solution.py:296
  25.8 7.3 %collective-permute-start.2 = (bf16[64,512]{1,0:T(8,128)(2,1)S(1)}, bf16[64,512]{1,0:T(8,128)(2,1)S(1)}, u32[]{:S(2)}, u32[]{:S(2)}) collective-permute-start(bf16[64,512]{1,0:T(8,128)(2,1)S(1)} %get-tuple-element.75), channel_id=1, source_target_pairs={{0,1},{1,2},{2,3},{3,4},{4,5},{5,6},{6,7},{7,8},{8,9},{9,10},{10,1... | collective-permute-start | bytes 196616 | tf_op jit(solution)/shard_map/ppermute | solution.py:295
  32.9 0.6 copy-start.7
  33.1 0.6 copy-start.9
  43.9 0.8 copy-start.5
  43.9 5.0 %copy-start.4 = (bf16[64,512]{1,0:T(8,128)(2,1)S(1)}, bf16[64,512]{1,0:T(8,128)(2,1)}, u32[]{:S(2)}) copy-start(bf16[64,512]{1,0:T(8,128)(2,1)} %get-tuple-element.49) | copy-start | bytes 196612
  43.9 136.8 %reduce-scatter.3.cloned.1.call-start = ((), (), s32[]{:S(2)}) async-start(), calls=%async_computation.2 | async-start | bytes 2367488 | tf_op jit(solution)/shard_map/reduce_scatter | solution.py:395
  44.7 5.5 %collective-permute-start.4 = (bf16[64,512]{1,0:T(8,128)(2,1)S(1)}, bf16[64,512]{1,0:T(8,128)(2,1)S(1)}, u32[]{:S(2)}, u32[]{:S(2)}) collective-permute-start(bf16[64,512]{1,0:T(8,128)(2,1)S(1)} %copy-done.5), channel_id=1, source_target_pairs={{0,1},{1,2},{2,3},{3,4},{4,5},{5,6},{6,7},{7,8},{8,9},{9,10},{10,1... | collective-permute-start | bytes 196616 | tf_op jit(solution)/shard_map/ppermute | solution.py:295
  48.9 5.0 %collective-permute-start.5 = (bf16[64,512]{1,0:T(8,128)(2,1)S(1)}, bf16[64,512]{1,0:T(8,128)(2,1)S(1)}, u32[]{:S(2)}, u32[]{:S(2)}) collective-permute-start(bf16[64,512]{1,0:T(8,128)(2,1)S(1)} %copy-done.4), channel_id=1, source_target_pairs={{1,0},{2,1},{3,2},{4,3},{5,4},{6,5},{7,6},{8,7},{9,8},{10,9},{11,1... | collective-permute-start | bytes 196616 | tf_op jit(solution)/shard_map/ppermute | solution.py:296
  50.2 3.7 %copy-start.6 = (bf16[64,512]{1,0:T(8,128)(2,1)}, bf16[64,512]{1,0:T(8,128)(2,1)S(1)}, u32[]{:S(2)}) copy-start(bf16[64,512]{1,0:T(8,128)(2,1)S(1)} %collective-permute-done.4.back_lo) | copy-start | bytes 196612
  53.9 0.6 copy-start.8
  63.2 1.0 copy-start.3
  63.2 5.9 %copy-start.2 = (bf16[256,512]{1,0:T(8,128)(2,1)S(1)}, bf16[256,512]{1,0:T(8,128)(2,1)}, u32[]{:S(2)}) copy-start(bf16[256,512]{1,0:T(8,128)(2,1)} %get-tuple-element.56) | copy-start | bytes 786436
  64.2 6.3 %collective-permute-start.6 = (bf16[256,512]{1,0:T(8,128)(2,1)S(1)}, bf16[256,512]{1,0:T(8,128)(2,1)S(1)}, u32[]{:S(2)}, u32[]{:S(2)}) collective-permute-start(bf16[256,512]{1,0:T(8,128)(2,1)S(1)} %copy-done.3), channel_id=1, source_target_pairs={{0,1},{1,2},{2,3},{3,4},{4,5},{5,6},{6,7},{7,8},{8,9},{9,10},{10,1... | collective-permute-start | bytes 786440 | tf_op jit(solution)/shard_map/ppermute | solution.py:295
  69.1 4.0 %collective-permute-start.7 = (bf16[256,512]{1,0:T(8,128)(2,1)S(1)}, bf16[256,512]{1,0:T(8,128)(2,1)S(1)}, u32[]{:S(2)}, u32[]{:S(2)}) collective-permute-start(bf16[256,512]{1,0:T(8,128)(2,1)S(1)} %copy-done.2), channel_id=1, source_target_pairs={{1,0},{2,1},{3,2},{4,3},{5,4},{6,5},{7,6},{8,7},{9,8},{10,9},{11,1... | collective-permute-start | bytes 786440 | tf_op jit(solution)/shard_map/ppermute | solution.py:296
Sparse Core Ops, SparseCore 0:
  44.0 70.9 reduce-scatter.4
  119.2 61.4 reduce-scatter.2
where the time goes:
time: 193 us; the launch traced here: 192 us
  waiting for transfers between devices  111 us (58%)
  Pallas kernels  25.3 us (13%)
  starting transfers between devices  23.8 us (12%)
  between operations  15.5 us (8%)
  other arithmetic  8.19 us (4%)
  local copies, waits for them, and re-layouts  8.02 us (4%)
    reduce_scatter x1, waiting for transfers between devices, per_device(): enc_sum = lax.psum_scatter(enc_w, 'space', scatter_dimension=0, tiled=True)  65.8 us
    reduce_scatter x1, waiting for transfers between devices, per_device(): lax.psum_scatter(proc_w, 'space', scatter_dimension=0, tiled=True)  40.2 us
    ppermute x4, starting transfers between devices, shift(): lax.ppermute(up, axis, [(i, i + 1) for i in range(ends)])  18.6 us
    pallas_call x1, Pallas kernels, per_device(): call(proc_kernel, [smem] * 3 + [vmem] * 4 + [layer_spec(1, matrices.shape...  10.1 us
    pallas_call x1, Pallas kernels, per_device(): call(enc_backward_kernel, [smem] * 3 + [vmem] * 8 + [layer_spec(0, matric...  8.66 us
    pallas_call x1, Pallas kernels, per_device(): call(enc_forward_kernel, [smem] * 3 + [hbm] * 3 + [vmem, layer_spec(0, ma...  6.53 us
    ppermute x4, starting transfers between devices, shift(): lax.ppermute(down, axis, [(i + 1, i) for i in range(ends)])  5.17 us
    ppermute x4, waiting for transfers between devices, shift(): lax.ppermute(down, axis, [(i + 1, i) for i in range(ends)])  4.63 us
  transfers between devices with their start and end apart: 10, of which 5 were waited for; matrix products, arithmetic and copies ran while one was open for 3% of the time, Pallas kernels for 5%

commit v1 on v0

--- a/solution.py
+++ b/solution.py
@@ -101,11 +101,35 @@
     return (du * (s + u * (1.0 - s))).astype(bf16), d_gain
 
 
-def write_small(w_ref, d_emb, d_gain):
+def halving_order(parts, layer):
+    order = list(range(parts.bit_length() - 1))
+    if layer == 0 and len(order) > 2:
+        order[1], order[2] = order[2], order[1]
+    return order
+
+
+def shard_at(place, parts, layer):
+    order = halving_order(parts, layer)
+    slab = 0
+    for k, bit in enumerate(order):
+        slab += ((place >> (len(order) - 1 - k)) & 1) << bit
+    return slab
+
+
+def write_shards(w_ref, layer, column, value):
+    parts, rows, _ = w_ref.shape
+    for place in range(parts):
+        slab = shard_at(place, parts, layer)
+        w_ref[place, :, column : column + value.shape[1]] = value[
+            slab * rows : (slab + 1) * rows, :
+        ].astype(bf16)
+
+
+def write_small(w_ref, layer, d_emb, d_gain):
     width = d_emb.shape[1]
     pad = jnp.zeros((SMALL - 16 - 8, width), f32)
     block = jnp.concatenate([d_emb, jnp.broadcast_to(d_gain, (8, width)), pad], axis=0)
-    w_ref[:, 4 * width :] = block.T.astype(bf16)
+    write_shards(w_ref, layer, 4 * width, block.T)
 
 
 def enc_forward_kernel(
@@ -211,11 +235,11 @@
     d_latent[...] = (
         cot32 + dot_tb(g, w[0, 2]) + dot_tb(d_recv, w[0, 1]) + d_rows[HM : HM + rows, :]
     )
-    w_out[:, 0:width] = dot_ta(d_send, ext[...]).astype(bf16)
-    w_out[:, width : 2 * width] = dot_ta(d_recv, latent).astype(bf16)
-    w_out[:, 2 * width : 3 * width] = dot_ta(g, latent).astype(bf16)
-    w_out[:, 3 * width : 4 * width] = dot_ta(g, agg).astype(bf16)
-    write_small(w_out, d_emb_acc[...], d_gain)
+    write_shards(w_out, 1, 0, dot_ta(d_send, ext[...]))
+    write_shards(w_out, 1, width, dot_ta(d_recv, latent))
+    write_shards(w_out, 1, 2 * width, dot_ta(g, latent))
+    write_shards(w_out, 1, 3 * width, dot_ta(g, agg))
+    write_small(w_out, 1, d_emb_acc[...], d_gain)
 
 
 def enc_backward_kernel(
@@ -259,11 +283,11 @@
     grid_own[...] = grid_acc[HG : HG + own, :].astype(bf16)
     d_recv = acc[...].astype(bf16)
     mesh_grad[...] = (cot + dot_tb(g, w[0, 2]) + dot_tb(d_recv, w[0, 1])).astype(bf16)
-    w_out[:, 0:width] = w0_acc[...].astype(bf16)
-    w_out[:, width : 2 * width] = dot_ta(d_recv, latent[...]).astype(bf16)
-    w_out[:, 2 * width : 3 * width] = dot_ta(g, latent[...]).astype(bf16)
-    w_out[:, 3 * width : 4 * width] = dot_ta(g, agg[...]).astype(bf16)
-    write_small(w_out, d_emb_acc[...], d_gain)
+    write_shards(w_out, 0, 0, w0_acc[...])
+    write_shards(w_out, 0, width, dot_ta(d_recv, latent[...]))
+    write_shards(w_out, 0, 2 * width, dot_ta(g, latent[...]))
+    write_shards(w_out, 0, 3 * width, dot_ta(g, agg[...]))
+    write_small(w_out, 0, d_emb_acc[...], d_gain)
 
 
 smem = pl.BlockSpec(memory_space=pltpu.SMEM)
@@ -289,12 +313,173 @@
     )
 
 
-def shift(up, down, axis):
-    ends = lax.axis_size(axis) - 1
-    return (
-        lax.ppermute(up, axis, [(i, i + 1) for i in range(ends)]),
-        lax.ppermute(down, axis, [(i + 1, i) for i in range(ends)]),
-    )
+def greet(targets):
+    barrier = pltpu.get_barrier_semaphore()
+    for slab, there in targets:
+
+        @pl.when(there)
+        def _(slab=slab):
+            pl.semaphore_signal(
+                barrier, inc=1, device_id={"space": slab}, device_id_type=pl.DeviceIdType.MESH
+            )
+
+    pl.semaphore_wait(barrier, sum(jnp.where(there, 1, 0) for _, there in targets))
+
+
+def remote(src, dst, send_sem, recv_sem, slab):
+    return pltpu.make_async_remote_copy(
+        src_ref=src,
+        dst_ref=dst,
+        send_sem=send_sem,
+        recv_sem=recv_sem,
+        device_id={"space": slab},
+        device_id_type=pl.DeviceIdType.MESH,
+    )
+
+
+def neighbours(parts):
+    me = lax.axis_index("space")
+    has_prev, has_next = me > 0, me < parts - 1
+    return jnp.maximum(me - 1, 0), jnp.minimum(me + 1, parts - 1), has_prev, has_next
+
+
+def start_halo(parts, up, down, from_prev, from_next, send_sem, recv_sem):
+    prev, after, has_prev, has_next = neighbours(parts)
+
+    @pl.when(has_next)
+    def _():
+        remote(up, from_prev, send_sem.at[0], recv_sem.at[0], after).start()
+
+    @pl.when(has_prev)
+    def _():
+        remote(down, from_next, send_sem.at[1], recv_sem.at[1], prev).start()
+
+    @pl.when(jnp.logical_not(has_prev))
+    def _():
+        from_prev[...] = jnp.zeros_like(from_prev)
+
+    @pl.when(jnp.logical_not(has_next))
+    def _():
+        from_next[...] = jnp.zeros_like(from_next)
+
+
+def finish_halo(parts, up, down, from_prev, from_next, send_sem, recv_sem):
+    prev, after, has_prev, has_next = neighbours(parts)
+
+    @pl.when(has_next)
+    def _():
+        remote(up, from_prev, send_sem.at[0], recv_sem.at[0], after).wait_send()
+        remote(down, from_next, send_sem.at[1], recv_sem.at[1], after).wait_recv()
+
+    @pl.when(has_prev)
+    def _():
+        remote(down, from_next, send_sem.at[1], recv_sem.at[1], prev).wait_send()
+        remote(up, from_prev, send_sem.at[0], recv_sem.at[0], prev).wait_recv()
+
+
+def exchange_kernel(parts, up, down, from_prev, from_next, send_sem, recv_sem):
+    prev, after, has_prev, has_next = neighbours(parts)
+    greet([(prev, has_prev), (after, has_next)])
+    refs = (up, down, from_prev, from_next, send_sem, recv_sem)
+    start_halo(parts, *refs)
+    finish_halo(parts, *refs)
+
+
+def exchange(parts, up, down, width, margin, up_block, down_block, collective_id):
+    return pl.pallas_call(
+        functools.partial(exchange_kernel, parts),
+        grid=(1,),
+        in_specs=[
+            pl.BlockSpec((margin, width), lambda i: (up_block, 0)),
+            pl.BlockSpec((margin, width), lambda i: (down_block, 0)),
+        ],
+        out_specs=[vmem] * 2,
+        out_shape=[jax.ShapeDtypeStruct((margin, width), bf16)] * 2,
+        scratch_shapes=[pltpu.SemaphoreType.DMA((2,)), pltpu.SemaphoreType.DMA((2,))],
+        compiler_params=pltpu.CompilerParams(collective_id=collective_id, has_side_effects=True),
+    )(up, down)
+
+
+def reduce_kernel(parts, enc_w, proc_w, up, down, enc_out, proc_out, from_prev, from_next, *scratch):
+    halo_send, halo_recv, send_sem, recv_sem = scratch[-4:]
+    stages = parts.bit_length() - 1
+    landing = [scratch[0:stages], scratch[stages : 2 * stages]]
+    kept = [scratch[2 * stages : 3 * stages - 1], scratch[3 * stages - 1 : 4 * stages - 2]]
+    outs = [enc_out, proc_out]
+    current = [enc_w, proc_w]
+    me = lax.axis_index("space")
+
+    def bit_of(bit):
+        return (me // (1 << bit)) % 2
+
+    prev, after, has_prev, has_next = neighbours(parts)
+    greet(
+        [(me + (1 - 2 * bit_of(bit)) * (1 << bit), me >= 0) for bit in range(stages)]
+        + [(prev, has_prev), (after, has_next)]
+    )
+
+    def copy_of(layer, stage):
+        bit = halving_order(parts, layer)[stage]
+        half = parts >> (stage + 1)
+        mine = bit_of(bit)
+        return remote(
+            current[layer].at[pl.ds((1 - mine) * half, half)],
+            landing[layer][stage],
+            send_sem.at[layer, stage],
+            recv_sem.at[layer, stage],
+            me + (1 - 2 * mine) * (1 << bit),
+        )
+
+    refs = (up, down, from_prev, from_next, halo_send, halo_recv)
+    copies = [copy_of(1, 0), copy_of(0, 0)]
+    copies[0].start()
+    copies[1].start()
+    start_halo(parts, *refs)
+    for stage in range(stages):
+        for slot, layer in ((0, 1), (1, 0)):
+            half = parts >> (stage + 1)
+            mine = bit_of(halving_order(parts, layer)[stage])
+            copies[slot].wait()
+            source, arrived = current[layer], landing[layer][stage]
+            if stage == stages - 1:
+                outs[layer][...] = source[mine].astype(f32) + arrived[0].astype(f32)
+                continue
+            target = kept[layer][stage]
+
+            def add(k, carry, source=source, arrived=arrived, target=target, mine=mine, half=half):
+                target[k] = (source[mine * half + k].astype(f32) + arrived[k].astype(f32)).astype(bf16)
+                return carry
+
+            lax.fori_loop(0, half, add, 0)
+            current[layer] = target
+            copies[slot] = copy_of(layer, stage + 1)
+            copies[slot].start()
+    finish_halo(parts, *refs)
+
+
+def reduce_weights(parts, enc_w, proc_w, up, down):
+    _, rows, columns = enc_w.shape
+    stages = parts.bit_length() - 1
+    landing = [pltpu.VMEM((parts >> (s + 1), rows, columns), bf16) for s in range(stages)]
+    kept = [pltpu.VMEM((parts >> (s + 1), rows, columns), bf16) for s in range(stages - 1)]
+    sds = jax.ShapeDtypeStruct
+    return pl.pallas_call(
+        functools.partial(reduce_kernel, parts),
+        in_specs=[vmem] * 4,
+        out_specs=[vmem] * 4,
+        out_shape=[sds((rows, columns), f32)] * 2 + [sds(up.shape, bf16)] * 2,
+        scratch_shapes=landing * 2
+        + kept * 2
+        + [
+            pltpu.SemaphoreType.DMA((2,)),
+            pltpu.SemaphoreType.DMA((2,)),
+            pltpu.SemaphoreType.DMA((2, stages)),
+            pltpu.SemaphoreType.DMA((2, stages)),
+        ],
+        compiler_params=pltpu.CompilerParams(
+            collective_id=3, has_side_effects=True, vmem_limit_bytes=VMEM_LIMIT
+        ),
+    )(enc_w, proc_w, up, down)
 
 
 def split_rows(a, axis, order):
@@ -310,6 +495,7 @@
     enc_recv_slot, enc_count, proc_send_block, proc_recv_block, proc_send_slot,
     proc_recv_slot, proc_count,
 ):
+    parts = lax.axis_size("space")
     rows, width = mesh_latent.shape
     own = grid_latent.shape[0]
     blocks = enc_send_block.shape[0]
@@ -319,7 +505,7 @@
     enc_attr = split_rows(enc_attributes, 0, (1, 0, 1))
     proc_attr = split_rows(proc_attributes, 0, (1, 0, 1))
 
-    lo, hi = shift(grid_latent[own - HG :], grid_latent[:HG], "space")
+    lo, hi = exchange(parts, grid_latent, grid_latent, width, HG, own // HG - 1, 0, 0)
     enc_out, agg, mixed, slopes, tiles = call(
         enc_forward_kernel,
         [smem] * 3 + [hbm] * 3 + [vmem, layer_spec(0, matrices.shape), vmem, layer_spec(0, emb.shape), vmem, vmem, vmem],
@@ -341,7 +527,7 @@
         norm_gains, emb, enc_attr, enc_send_slot, enc_recv_slot,
     )
 
-    lo, hi = shift(enc_out[rows - HM :], enc_out[:HM], "space")
+    lo, hi = exchange(parts, enc_out, enc_out, width, HM, rows // HM - 1, 0, 1)
     mesh_out, d_latent, rim_lo, rim_hi, proc_w = call(
         proc_kernel,
         [smem] * 3 + [vmem] * 4 + [layer_spec(1, matrices.shape), vmem, layer_spec(1, emb.shape), vmem, vmem, vmem],
@@ -350,7 +536,7 @@
             sds((rows, width), f32),
             sds((HM, width), bf16),
             sds((HM, width), bf16),
-            sds((width, 4 * width + SMALL), bf16),
+            sds((parts, width // parts, 4 * width + SMALL), bf16),
         ],
         [
             pltpu.VMEM((rows + 2 * HM, width), bf16),
@@ -366,8 +552,7 @@
         norm_gains, emb, proc_attr, proc_send_slot, proc_recv_slot,
     )
 
-    back_lo, back_hi = shift(rim_hi, rim_lo, "space")
-    proc_sum = lax.psum_scatter(proc_w, "space", scatter_dimension=0, tiled=True)
+    back_lo, back_hi = exchange(parts, rim_hi, rim_lo, width, HM, 0, 0, 2)
     mesh_grad, grid_own, grid_lo, grid_hi, enc_w = call(
         enc_backward_kernel,
         [smem] * 3 + [vmem] * 8 + [layer_spec(0, matrices.shape), vmem, vmem, vmem, vmem],
@@ -376,7 +561,7 @@
             sds((own, width), bf16),
             sds((HG, width), bf16),
             sds((HG, width), bf16),
-            sds((width, 4 * width + SMALL), bf16),
+            sds((parts, width // parts, 4 * width + SMALL), bf16),
         ],
         [
             pltpu.VMEM((own + 2 * HG, width), f32),
@@ -390,11 +575,10 @@
         enc_send_block, enc_recv_block, enc_count, d_latent, back_lo, back_hi, mesh_latent, agg,
         mixed, slopes, tiles, matrices, norm_gains, enc_attr, enc_send_slot, enc_recv_slot,
     )
-    from_prev, from_next = shift(grid_hi, grid_lo, "space")
+    enc_sum, proc_sum, from_prev, from_next = reduce_weights(parts, enc_w, proc_w, grid_hi, grid_lo)
     grid_grad = grid_own.at[:HG].add(from_prev).at[own - HG :].add(from_next)
-    enc_sum = lax.psum_scatter(enc_w, "space", scatter_dimension=0, tiled=True)
-
-    sums = jnp.stack([enc_sum, proc_sum]).astype(f32)
+
+    sums = jnp.stack([enc_sum, proc_sum])
     columns = sums.shape[1]
     matrix_grads = sums[:, :, : 4 * width].reshape(2, columns, 4, width).transpose(0, 2, 3, 1)
     small = sums[:, :, 4 * width :].transpose(0, 2, 1)

time: 193 us -> 111 us (0.58)
  waiting for transfers between devices: 111 us -> 0 us
  Pallas kernels: 25.3 us -> 97.8 us
  starting transfers between devices: 23.8 us -> 0 us
  between operations: 15.5 us -> 2 us
  local copies, waits for them, and re-layouts: 8.02 us -> 2.33 us
    reduce_scatter x2 -> x0, waiting for transfers between devices: 106 us -> none  [the longest x1 65.8 us: per_device(): enc_sum = lax.psum_scatter(enc_w, 'space', scatter_dimension=0, tiled=True)]
    pallas_call x0 -> x4, Pallas kernels: none -> 72.1 us  [the longest x1 50.7 us: reduce_weights(): pl.pallas_call(functools.partial(reduce_kernel, parts), in_specs=[vmem] *...]
    ppermute x8 -> x0, starting transfers between devices: 23.8 us -> none  [the longest x4 18.6 us: shift(): lax.ppermute(up, axis, [(i, i + 1) for i in range(ends)])]
    ppermute x8 -> x0, waiting for transfers between devices: 4.85 us -> none  [the longest x4 4.63 us: shift(): lax.ppermute(down, axis, [(i + 1, i) for i in range(ends)])]
    unnamed x21 -> x5, local copies, waits for them, and re-layouts: 4.39 us -> 0.69 us
    slice x3 -> x0, local copies, waits for them, and re-layouts: 1.98 us -> none  [the longest x1 1.07 us: per_device(): lo, hi = shift(grid_latent[own - HG:], grid_latent[:HG], 'space')]
  transfers between devices with their start and end apart: 10 -> 0, of which waited for: 5 -> 0; matrix products, arithmetic and copies ran while one was open for 3% -> 0% of each run, Pallas kernels for 5% -> 0%
where the time goes in v1:
time: 111 us; the launch traced here: 110 us
  Pallas kernels  97.8 us (88%)
  other arithmetic  7.42 us (7%)
  local copies, waits for them, and re-layouts  2.33 us (2%)
  between operations  2 us (2%)
    pallas_call x1, Pallas kernels, reduce_weights(): pl.pallas_call(functools.partial(reduce_kernel, parts), in_specs=[vmem] *...  50.7 us
    pallas_call x3, Pallas kernels, exchange(): pl.pallas_call(functools.partial(exchange_kernel, parts), grid=(1,), in_s...  21.3 us
    pallas_call x1, Pallas kernels, per_device(): call(enc_backward_kernel, [smem] * 3 + [vmem] * 8 + [layer_spec(0, matric...  9.67 us
    pallas_call x1, Pallas kernels, per_device(): call(proc_kernel, [smem] * 3 + [vmem] * 4 + [layer_spec(1, matrices.shape...  8.32 us
    pallas_call x1, Pallas kernels, per_device(): call(enc_forward_kernel, [smem] * 3 + [hbm] * 3 + [vmem, layer_spec(0, ma...  7.71 us
    scatter-add x2, other arithmetic, per_device(): grid_grad = grid_own.at[:HG].add(from_prev).at[own - HG:].add(from_next)  3.65 us

profile of v1, /device:TPU:0, one launch (start us, length us, event | category | flops | bytes accessed | tf_op | source)
XLA Modules:
  0.0 109.5 jit_solution(267651229454601032)
XLA Ops:
  1.9 0.1 pad.17.clone
  2.0 0.7 reduce-precision_convert_fusion.2
  2.7 0.7 maximum_maximum_fusion.2.emb
  3.4 0.8 fusion.2
  4.2 0.7 maximum_maximum_fusion.1
  4.9 6.0 %shard_map.217 = (bf16[256,512]{1,0:T(8,128)(2,1)}, bf16[256,512]{1,0:T(8,128)(2,1)}) custom-call(bf16[2048,512]{1,0:T(8,128)(2,1)} %own.1, bf16[2048,512]{1,0:T(8,128)(2,1)} %own.1), custom_call_target="tpu_custom_call" | custom-call | tf_op jit(solution)/shard_map/pallas_call | solution.py:389
  10.9 7.7 %shard_map.218 = (bf16[256,512]{1,0:T(8,128)(2,1)}, bf16[256,512]{1,0:T(8,128)(2,1)}, f32[256,512]{1,0:T(8,128)}, bf16[2048,512]{1,0:T(8,128)(2,1)}, bf16[1024,512]{1,0:T(8,128)(2,1)}) custom-call(s32[16]{0:T(128)} %send_block.5, s32[16]{0:T(128)} %recv_block.5, s32[1]{0:T(128)S(6)} %copy.33.count, bf16[2048,512]{1,0:T(8,128)(2,1)} %own.1, ...), custom_call_target="tpu_custom_call" | custom-call | flops 4000000000 | bytes 10000000 | tf_op jit(solution)/shard_map/pallas_call | solution.py:509
  18.6 9.9 %shard_map.219 = (bf16[64,512]{1,0:T(8,128)(2,1)}, bf16[64,512]{1,0:T(8,128)(2,1)}) custom-call(bf16[256,512]{1,0:T(8,128)(2,1)} %get-tuple-element.57.up.down.enc_out, bf16[256,512]{1,0:T(8,128)(2,1)} %get-tuple-element.57.up.down.enc_out), custom_call_target="tpu_custom_call" | custom-call | tf_op jit(solution)/shard_map/pallas_call | solution.py:389
  28.5 8.3 %shard_map.220 = (bf16[256,512]{1,0:T(8,128)(2,1)}, f32[256,512]{1,0:T(8,128)}, bf16[64,512]{1,0:T(8,128)(2,1)}, bf16[64,512]{1,0:T(8,128)(2,1)}, bf16[16,32,2176]{2,1,0:T(8,128)(2,1)}) custom-call(s32[16]{0:T(128)} %send_block.4, s32[16]{0:T(128)} %recv_block.4, s32[1]{0:T(128)S(6)} %copy.34.count, bf16[256,512]{1,0:T(8,128)(2,1)} %get-tuple-element.57.up.down.enc_out, ...), custom_call_target="tpu_custom_call" | custom-call | flops 8000000000 | bytes 10000000 | tf_op jit(solution)/shard_map/pallas_call | solution.py:531
  36.9 5.5 %shard_map.221 = (bf16[64,512]{1,0:T(8,128)(2,1)}, bf16[64,512]{1,0:T(8,128)(2,1)}) custom-call(bf16[64,512]{1,0:T(8,128)(2,1)} %get-tuple-element.62.up, bf16[64,512]{1,0:T(8,128)(2,1)} %get-tuple-element.63.down), custom_call_target="tpu_custom_call" | custom-call | tf_op jit(solution)/shard_map/pallas_call | solution.py:389
  42.3 9.7 %shard_map.222 = (bf16[256,512]{1,0:T(8,128)(2,1)}, bf16[2048,512]{1,0:T(8,128)(2,1)}, bf16[256,512]{1,0:T(8,128)(2,1)}, bf16[256,512]{1,0:T(8,128)(2,1)}, bf16[16,32,2176]{2,1,0:T(8,128)(2,1)}) custom-call(s32[16]{0:T(128)} %send_block.5, s32[16]{0:T(128)} %recv_block.5, s32[1]{0:T(128)S(6)} %copy.33.count, f32[256,512]{1,0:T(8,128)} %get-tuple-element.61.d_latent, ...), custom_call_target="tpu_custom_call" | custom-call | flops 8000000000 | bytes 10000000 | tf_op jit(solution)/shard_map/pallas_call | solution.py:556
  52.0 50.7 %shard_map.223 = (f32[32,2176]{1,0:T(8,128)}, f32[32,2176]{1,0:T(8,128)}, bf16[256,512]{1,0:T(8,128)(2,1)}, bf16[256,512]{1,0:T(8,128)(2,1)}) custom-call(bf16[16,32,2176]{2,1,0:T(8,128)(2,1)} %get-tuple-element.71.enc_w, bf16[16,32,2176]{2,1,0:T(8,128)(2,1)} %get-tuple-element.72.proc_w, bf16[256,512]{1,0:T(8,128)(2,1)} %get-tuple-element.73.up, ...), custom_call_target="tpu_custom_call" | custom-call | tf_op jit(solution)/shard_map/pallas_call | solution.py:466
  102.8 0.0 copy-start
  102.8 0.0 copy-start.1
  102.8 1.9 %add_dynamic-update-slice_fusion = bf16[2048,512]{1,0:T(8,128)(2,1)} fusion(bf16[2048,512]{1,0:T(8,128)(2,1)} %get-tuple-element.70, bf16[256,512]{1,0:T(8,128)(2,1)} %get-tuple-element.75), kind=kLoop, calls=%fused_computation.6 | loop fusion | flops 524288 | bytes 786432 | tf_op jit(solution)/shard_map/scatter-add | solution.py:579
  104.6 1.8 %fusion.1 = bf16[2048,512]{1,0:T(8,128)(2,1)} fusion(bf16[2048,512]{1,0:T(8,128)(2,1)} %add_dynamic-update-slice_fusion, bf16[256,512]{1,0:T(8,128)(2,1)} %get-tuple-element.76), kind=kLoop, calls=%fused_computation.5 | loop fusion | flops 524288 | bytes 786432 | tf_op jit(solution)/shard_map/scatter-add | solution.py:579
  106.4 0.7 fusion.4
  107.2 0.0 copy-done
  107.2 0.0 copy-done.1
  107.2 0.8 copy.30
  108.0 0.7 slice_reduce_fusion
  108.8 0.1 slice_add_fusion.1
  108.8 0.7 copy.27
  (2 shorter events, 0.0 us)
Async XLA Ops:
  102.8 4.4 %copy-start = (f32[32,2176]{1,0:T(8,128)S(1)}, f32[32,2176]{1,0:T(8,128)}, u32[]{:S(2)}) copy-start(f32[32,2176]{1,0:T(8,128)} %get-tuple-element.78) | copy-start | bytes 835588
  102.8 4.4 %copy-start.1 = (f32[32,2176]{1,0:T(8,128)S(1)}, f32[32,2176]{1,0:T(8,128)}, u32[]{:S(2)}) copy-start(f32[32,2176]{1,0:T(8,128)} %get-tuple-element.79) | copy-start | bytes 835588

commit v2 on v1

--- a/solution.py
+++ b/solution.py
@@ -166,6 +166,11 @@
             slope_out[group * GE : (group + 1) * GE, :] = slope
             acc[...] += summed
 
+        @pl.when(group * GB >= count[0])
+        def _(group=group):
+            for ref, size in ((slope_out, GE), (tiles_out, GB * BLK)):
+                ref[group * size : (group + 1) * size, :] = jnp.zeros((size, ref.shape[1]), bf16)
+
     agg = acc[...].astype(bf16)
     agg_out[...] = agg
     mixed = dot(latent[...], w[0, 2]) + dot(agg, w[0, 3])
@@ -242,54 +247,6 @@
     write_small(w_out, 1, d_emb_acc[...], d_gain)
 
 
-def enc_backward_kernel(
-    send_block, recv_block, count, d_latent, back_lo, back_hi, latent, agg, mixed, slopes, tiles,
-    w, gains, attr, send_slot, recv_slot,
-    mesh_grad, grid_own, grid_lo, grid_hi, w_out, grid_acc, acc, d_emb_acc, w0_acc, cot_ref,
-):
-    rows, width = latent.shape
-    groups = send_slot.shape[0] // GB
-    cot_ref[...] = d_latent[...]
-    cot_ref[0:HM, :] += back_lo[...].astype(f32)
-    cot_ref[rows - HM :, :] += back_hi[...].astype(f32)
-    cot = cot_ref[...].astype(bf16).astype(f32)
-    g, d_gain = tail_backward(mixed[...], cot, gains[0:1, :])
-    d_agg = dot_tb(g, w[0, 3]).astype(bf16)
-    cols_r = recv_slot[...].T
-    grid_acc[...] = jnp.zeros_like(grid_acc)
-    acc[...] = jnp.zeros_like(acc)
-    d_emb_acc[...] = jnp.zeros_like(d_emb_acc)
-    w0_acc[...] = jnp.zeros_like(w0_acc)
-    for group in range(groups):
-
-        @pl.when(group * GB < count[0])
-        def _(group=group):
-            d_send, d_recv, d_emb = edges_backward(
-                group, d_agg, slopes[group * GE : (group + 1) * GE, :], cols_r, send_slot,
-                recv_slot, recv_block, attr,
-            )
-            d_send = d_send.astype(bf16)
-            d_rows = dot_tb(d_send, w[0, 0])
-            for m in range(GB):
-                start = pl.multiple_of(send_block[group * GB + m] * BLK, BLK)
-                grid_acc[pl.ds(start, BLK), :] += d_rows[m * BLK : (m + 1) * BLK, :]
-            acc[...] += d_recv
-            d_emb_acc[...] += d_emb
-            w0_acc[...] += dot_ta(d_send, tiles[group * GB * BLK : (group + 1) * GB * BLK, :])
-
-    own = grid_own.shape[0]
-    grid_lo[...] = grid_acc[0:HG, :].astype(bf16)
-    grid_hi[...] = grid_acc[HG + own :, :].astype(bf16)
-    grid_own[...] = grid_acc[HG : HG + own, :].astype(bf16)
-    d_recv = acc[...].astype(bf16)
-    mesh_grad[...] = (cot + dot_tb(g, w[0, 2]) + dot_tb(d_recv, w[0, 1])).astype(bf16)
-    write_shards(w_out, 0, 0, w0_acc[...])
-    write_shards(w_out, 0, width, dot_ta(d_recv, latent[...]))
-    write_shards(w_out, 0, 2 * width, dot_ta(g, latent[...]))
-    write_shards(w_out, 0, 3 * width, dot_ta(g, agg[...]))
-    write_small(w_out, 0, d_emb_acc[...], d_gain)
-
-
 smem = pl.BlockSpec(memory_space=pltpu.SMEM)
 hbm = pl.BlockSpec(memory_space=pl.ANY)
 vmem = pl.BlockSpec(memory_space=pltpu.VMEM)
@@ -400,93 +357,167 @@
     )(up, down)
 
 
-def reduce_kernel(parts, enc_w, proc_w, up, down, enc_out, proc_out, from_prev, from_next, *scratch):
-    halo_send, halo_recv, send_sem, recv_sem = scratch[-4:]
+def row_places(send_block, blocks):
+    lanes = lax.broadcasted_iota(jnp.int32, (1, 2 * BLK), 1)
+    pairs = []
+    for b in range(0, blocks, 2):
+        first = send_block[b] * BLK
+        second = send_block[b + 1] * BLK - BLK
+        pairs.append(lanes + jnp.where(lanes < BLK, first, second))
+    return jnp.concatenate(pairs, axis=1)
+
+
+def enc_backward_kernel(
+    parts, send_block, recv_block, d_latent, rim_up, rim_down, latent, agg, mixed, slopes, tiles,
+    w, gains, attr, send_slot, recv_slot, proc_w,
+    mesh_grad, grid_grad, enc_out, proc_out,
+    back_lo, back_hi, grid_lo, grid_hi, from_prev, from_next, enc_w, d_rows, acc, d_emb_acc,
+    w0_acc, cot_ref, *scratch,
+):
+    rim_send, rim_recv, halo_send, halo_recv, send_sem, recv_sem = scratch[-6:]
     stages = parts.bit_length() - 1
     landing = [scratch[0:stages], scratch[stages : 2 * stages]]
     kept = [scratch[2 * stages : 3 * stages - 1], scratch[3 * stages - 1 : 4 * stages - 2]]
     outs = [enc_out, proc_out]
     current = [enc_w, proc_w]
+    copies = [None, None]
+    done = [0, 0]
     me = lax.axis_index("space")
 
     def bit_of(bit):
         return (me // (1 << bit)) % 2
 
-    prev, after, has_prev, has_next = neighbours(parts)
-    greet(
-        [(me + (1 - 2 * bit_of(bit)) * (1 << bit), me >= 0) for bit in range(stages)]
-        + [(prev, has_prev), (after, has_next)]
-    )
-
-    def copy_of(layer, stage):
+    def start(layer):
+        stage = done[layer]
         bit = halving_order(parts, layer)[stage]
         half = parts >> (stage + 1)
         mine = bit_of(bit)
-        return remote(
+        copies[layer] = remote(
             current[layer].at[pl.ds((1 - mine) * half, half)],
             landing[layer][stage],
             send_sem.at[layer, stage],
             recv_sem.at[layer, stage],
             me + (1 - 2 * mine) * (1 << bit),
         )
-
-    refs = (up, down, from_prev, from_next, halo_send, halo_recv)
-    copies = [copy_of(1, 0), copy_of(0, 0)]
-    copies[0].start()
-    copies[1].start()
+        copies[layer].start()
+
+    def advance(layer):
+        stage = done[layer]
+        if stage == stages:
+            return
+        half = parts >> (stage + 1)
+        mine = bit_of(halving_order(parts, layer)[stage])
+        copies[layer].wait()
+        source, arrived = current[layer], landing[layer][stage]
+        done[layer] += 1
+        if stage == stages - 1:
+            outs[layer][...] = source[mine].astype(f32) + arrived[0].astype(f32)
+            return
+        target = kept[layer][stage]
+
+        def add(k, carry):
+            target[k] = (source[mine * half + k].astype(f32) + arrived[k].astype(f32)).astype(bf16)
+            return carry
+
+        lax.fori_loop(0, half, add, 0)
+        current[layer] = target
+        start(layer)
+
+    prev, after, has_prev, has_next = neighbours(parts)
+    greet(
+        [(me + (1 - 2 * bit_of(bit)) * (1 << bit), me >= 0) for bit in range(stages)]
+        + [(prev, has_prev), (after, has_next)]
+    )
+    rims = (rim_up, rim_down, back_lo, back_hi, rim_send, rim_recv)
+    halos = (grid_hi, grid_lo, from_prev, from_next, halo_send, halo_recv)
+    start_halo(parts, *rims)
+    start(1)
+
+    rows, width = latent.shape
+    groups = send_slot.shape[0] // GB
+    cols_r = recv_slot[...].T
+    cot_ref[...] = d_latent[...]
+    acc[...] = jnp.zeros_like(acc)
+    d_emb_acc[...] = jnp.zeros_like(d_emb_acc)
+    w0_acc[...] = jnp.zeros_like(w0_acc)
+    finish_halo(parts, *rims)
+    cot_ref[0:HM, :] += back_lo[...].astype(f32)
+    cot_ref[rows - HM :, :] += back_hi[...].astype(f32)
+    cot = cot_ref[...].astype(bf16).astype(f32)
+    g, d_gain = tail_backward(mixed[...], cot, gains[0:1, :])
+    d_agg = dot_tb(g, w[0, 3]).astype(bf16)
+    write_shards(enc_w, 0, 2 * width, dot_ta(g, latent[...]))
+    write_shards(enc_w, 0, 3 * width, dot_ta(g, agg[...]))
+    for group in range(groups):
+        tile = pl.ds(group * GB * BLK, GB * BLK)
+        d_send, d_recv, d_emb = edges_backward(
+            group, d_agg, slopes[group * GE : (group + 1) * GE, :], cols_r, send_slot,
+            recv_slot, recv_block, attr,
+        )
+        d_send = d_send.astype(bf16)
+        d_rows[tile, :] = dot_tb(d_send, w[0, 0]).astype(bf16)
+        acc[...] += d_recv
+        d_emb_acc[...] += d_emb
+        w0_acc[...] += dot_ta(d_send, tiles[tile, :])
+        if group in (0, groups - 1):
+            advance(1)
+
+    d_recv = acc[...].astype(bf16)
+    write_shards(enc_w, 0, 0, w0_acc[...])
+    write_shards(enc_w, 0, width, dot_ta(d_recv, latent[...]))
+    write_small(enc_w, 0, d_emb_acc[...], d_gain)
+    start(0)
+
+    own = grid_grad.shape[0]
+    places = row_places(send_block, send_slot.shape[0])
+    ids = lax.broadcasted_iota(jnp.int32, (HG, places.shape[1]), 0)
+
+    def scattered(chunk):
+        return dot((ids + chunk * HG == places).astype(f32).astype(bf16), d_rows[...]).astype(bf16)
+
+    def own_chunk(chunk, carry):
+        grid_grad[pl.ds(pl.multiple_of(chunk * HG, HG), HG), :] = scattered(chunk + 1)
+        return carry
+
+    grid_lo[...] = scattered(0)
+    grid_hi[...] = scattered(own // HG + 1)
+    start_halo(parts, *halos)
+    middle = own // HG // 2
+    advance(0)
+    lax.fori_loop(0, middle, own_chunk, 0)
+    advance(1)
+    lax.fori_loop(middle, own // HG, own_chunk, 0)
+    mesh_grad[...] = (cot + dot_tb(g, w[0, 2]) + dot_tb(d_recv, w[0, 1])).astype(bf16)
+    for _ in range(stages):
+        advance(0)
+        advance(1)
+    finish_halo(parts, *halos)
+    grid_grad[0:HG, :] += from_prev[...]
+    grid_grad[own - HG :, :] += from_next[...]
+
+
+def first_exchange_kernel(
+    parts, up, down, enc_a, proc_a, emb, from_prev, from_next, enc_attr, proc_attr, emb_out,
+    wide, narrow, send_sem, recv_sem,
+):
+    prev, after, has_prev, has_next = neighbours(parts)
+    greet([(prev, has_prev), (after, has_next)])
+    refs = (up, down, from_prev, from_next, send_sem, recv_sem)
     start_halo(parts, *refs)
-    for stage in range(stages):
-        for slot, layer in ((0, 1), (1, 0)):
-            half = parts >> (stage + 1)
-            mine = bit_of(halving_order(parts, layer)[stage])
-            copies[slot].wait()
-            source, arrived = current[layer], landing[layer][stage]
-            if stage == stages - 1:
-                outs[layer][...] = source[mine].astype(f32) + arrived[0].astype(f32)
-                continue
-            target = kept[layer][stage]
-
-            def add(k, carry, source=source, arrived=arrived, target=target, mine=mine, half=half):
-                target[k] = (source[mine * half + k].astype(f32) + arrived[k].astype(f32)).astype(bf16)
-                return carry
-
-            lax.fori_loop(0, half, add, 0)
-            current[layer] = target
-            copies[slot] = copy_of(layer, stage + 1)
-            copies[slot].start()
+
+    def split(value, work, order):
+        top = value.astype(bf16).astype(f32)
+        rest = value - top
+        work[...] = jnp.zeros_like(work)
+        for k, high in enumerate(order):
+            work[4 * k : 4 * k + 4, :] = top if high else rest
+        return work[...].astype(bf16)
+
+    enc_attr[...] = split(enc_a[...], wide, (1, 0, 1))
+    proc_attr[...] = split(proc_a[...], wide, (1, 0, 1))
+    for layer in range(2):
+        emb_out[layer] = split(emb[layer], narrow, (1, 1, 0))
     finish_halo(parts, *refs)
-
-
-def reduce_weights(parts, enc_w, proc_w, up, down):
-    _, rows, columns = enc_w.shape
-    stages = parts.bit_length() - 1
-    landing = [pltpu.VMEM((parts >> (s + 1), rows, columns), bf16) for s in range(stages)]
-    kept = [pltpu.VMEM((parts >> (s + 1), rows, columns), bf16) for s in range(stages - 1)]
-    sds = jax.ShapeDtypeStruct
-    return pl.pallas_call(
-        functools.partial(reduce_kernel, parts),
-        in_specs=[vmem] * 4,
-        out_specs=[vmem] * 4,
-        out_shape=[sds((rows, columns), f32)] * 2 + [sds(up.shape, bf16)] * 2,
-        scratch_shapes=landing * 2
-        + kept * 2
-        + [
-            pltpu.SemaphoreType.DMA((2,)),
-            pltpu.SemaphoreType.DMA((2,)),
-            pltpu.SemaphoreType.DMA((2, stages)),
-            pltpu.SemaphoreType.DMA((2, stages)),
-        ],
-        compiler_params=pltpu.CompilerParams(
-            collective_id=3, has_side_effects=True, vmem_limit_bytes=VMEM_LIMIT
-        ),
-    )(enc_w, proc_w, up, down)
-
-
-def split_rows(a, axis, order):
-    top = lax.reduce_precision(a, 8, 7)
-    rest = a - top
-    pieces = [top if k else rest for k in order]
-    return jnp.concatenate(pieces + [jnp.zeros_like(a)], axis=axis).astype(bf16)
 
 
 def per_device(
@@ -501,11 +532,30 @@
     blocks = enc_send_block.shape[0]
     p_blocks = proc_send_block.shape[0]
     sds = jax.ShapeDtypeStruct
-    emb = split_rows(edge_embeddings, 1, (1, 1, 0))
-    enc_attr = split_rows(enc_attributes, 0, (1, 0, 1))
-    proc_attr = split_rows(proc_attributes, 0, (1, 0, 1))
-
-    lo, hi = exchange(parts, grid_latent, grid_latent, width, HG, own // HG - 1, 0, 0)
+
+    edges = enc_attributes.shape[1]
+    lo, hi, enc_attr, proc_attr, emb = pl.pallas_call(
+        functools.partial(first_exchange_kernel, parts),
+        grid=(1,),
+        in_specs=[
+            pl.BlockSpec((HG, width), lambda i: (own // HG - 1, 0)),
+            pl.BlockSpec((HG, width), lambda i: (0, 0)),
+        ]
+        + [vmem] * 3,
+        out_specs=[vmem] * 5,
+        out_shape=[sds((HG, width), bf16)] * 2
+        + [sds((16, edges), bf16)] * 2
+        + [sds((2, 16, width), bf16)],
+        scratch_shapes=[
+            pltpu.VMEM((16, edges), f32),
+            pltpu.VMEM((16, width), f32),
+            pltpu.SemaphoreType.DMA((2,)),
+            pltpu.SemaphoreType.DMA((2,)),
+        ],
+        compiler_params=pltpu.CompilerParams(
+            collective_id=0, has_side_effects=True, vmem_limit_bytes=VMEM_LIMIT
+        ),
+    )(grid_latent, grid_latent, enc_attributes, proc_attributes, edge_embeddings)
     enc_out, agg, mixed, slopes, tiles = call(
         enc_forward_kernel,
         [smem] * 3 + [hbm] * 3 + [vmem, layer_spec(0, matrices.shape), vmem, layer_spec(0, emb.shape), vmem, vmem, vmem],
@@ -552,31 +602,42 @@
         norm_gains, emb, proc_attr, proc_send_slot, proc_recv_slot,
     )
 
-    back_lo, back_hi = exchange(parts, rim_hi, rim_lo, width, HM, 0, 0, 2)
-    mesh_grad, grid_own, grid_lo, grid_hi, enc_w = call(
-        enc_backward_kernel,
-        [smem] * 3 + [vmem] * 8 + [layer_spec(0, matrices.shape), vmem, vmem, vmem, vmem],
-        [
+    stages = parts.bit_length() - 1
+    columns = 4 * width + SMALL
+    shard = width // parts
+    landing = [pltpu.VMEM((parts >> (k + 1), shard, columns), bf16) for k in range(stages)]
+    mesh_grad, grid_grad, enc_sum, proc_sum = pl.pallas_call(
+        functools.partial(enc_backward_kernel, parts),
+        grid=(1,),
+        in_specs=[smem] * 2 + [vmem] * 8 + [layer_spec(0, matrices.shape)] + [vmem] * 5,
+        out_specs=[vmem] * 4,
+        out_shape=[
             sds((rows, width), bf16),
             sds((own, width), bf16),
-            sds((HG, width), bf16),
-            sds((HG, width), bf16),
-            sds((parts, width // parts, 4 * width + SMALL), bf16),
+            sds((shard, columns), f32),
+            sds((shard, columns), f32),
         ],
-        [
-            pltpu.VMEM((own + 2 * HG, width), f32),
+        scratch_shapes=[pltpu.VMEM((HM, width), bf16)] * 2
+        + [pltpu.VMEM((HG, width), bf16)] * 4
+        + [
+            pltpu.VMEM((parts, shard, columns), bf16),
+            pltpu.VMEM((blocks * BLK, width), bf16),
             pltpu.VMEM((rows, width), f32),
             pltpu.VMEM((16, width), f32),
             pltpu.VMEM((width, width), f32),
             pltpu.VMEM((rows, width), f32),
-        ],
-        8_000_000_000,
+        ]
+        + landing * 2
+        + landing[:-1] * 2
+        + [pltpu.SemaphoreType.DMA((2,))] * 4
+        + [pltpu.SemaphoreType.DMA((2, stages))] * 2,
+        compiler_params=pltpu.CompilerParams(
+            collective_id=2, has_side_effects=True, vmem_limit_bytes=VMEM_LIMIT
+        ),
     )(
-        enc_send_block, enc_recv_block, enc_count, d_latent, back_lo, back_hi, mesh_latent, agg,
-        mixed, slopes, tiles, matrices, norm_gains, enc_attr, enc_send_slot, enc_recv_slot,
-    )
-    enc_sum, proc_sum, from_prev, from_next = reduce_weights(parts, enc_w, proc_w, grid_hi, grid_lo)
-    grid_grad = grid_own.at[:HG].add(from_prev).at[own - HG :].add(from_next)
+        enc_send_block, enc_recv_block, d_latent, rim_hi, rim_lo, mesh_latent, agg, mixed, slopes,
+        tiles, matrices, norm_gains, enc_attr, enc_send_slot, enc_recv_slot, proc_w,
+    )
 
     sums = jnp.stack([enc_sum, proc_sum])
     columns = sums.shape[1]

time: 111 us -> 112 us (level)
  other arithmetic: 7.42 us -> 2.03 us
  Pallas kernels: 97.8 us -> 103 us
  local copies, waits for them, and re-layouts: 2.33 us -> 4.27 us
    pallas_call x2, Pallas kernels: 60.4 us -> 77.2 us  [the longest x1 71.1 us: per_device(): pl.pallas_call(functools.partial(enc_backward_kernel, parts), grid=(1,),...]
    pallas_call x3 -> x1, Pallas kernels: 21.3 us -> 9.91 us  [exchange(): pl.pallas_call(functools.partial(exchange_kernel, parts), grid=(1,), in_s...]
    scatter-add x2 -> x0, other arithmetic: 3.65 us -> none  [per_device(): grid_grad = grid_own.at[:HG].add(from_prev).at[own - HG:].add(from_next)]
    unnamed x5 -> x7, local copies, waits for them, and re-layouts: 0.69 us -> 2.71 us
    another operation x2 -> x0, other arithmetic: 1.52 us -> none
    concatenate x2 -> x0, other arithmetic: 1.4 us -> none  [split_rows(): return jnp.concatenate(pieces + [jnp.zeros_like(a)], axis=axis).astype(bf16)]
    another operation x1, other arithmetic: 0.03 us -> 1.21 us  [per_device(): sums = jnp.stack([enc_sum, proc_sum])]
where the time goes in v2:
time: 112 us
  Pallas kernels  103 us (92%)
  local copies, waits for them, and re-layouts  4.27 us (4%)
  other arithmetic  2.03 us (2%)
  between operations  1.98 us (2%)
    pallas_call x1, Pallas kernels, per_device(): pl.pallas_call(functools.partial(enc_backward_kernel, parts), grid=(1,),...  71.1 us
    pallas_call x1, Pallas kernels, exchange(): pl.pallas_call(functools.partial(exchange_kernel, parts), grid=(1,), in_s...  9.91 us
    pallas_call x1, Pallas kernels, per_device(): call(proc_kernel, [smem] * 3 + [vmem] * 4 + [layer_spec(1, matrices.shape...  8.3 us
    pallas_call x1, Pallas kernels, per_device(): call(enc_forward_kernel, [smem] * 3 + [hbm] * 3 + [vmem, layer_spec(0, ma...  7.84 us
    pallas_call x1, Pallas kernels, per_device(): pl.pallas_call(functools.partial(first_exchange_kernel, parts), grid=(1,)...  6.08 us
    unnamed x7, local copies, waits for them, and re-layouts  2.71 us

profile of v2, /device:TPU:0, one launch (start us, length us, event | category | flops | bytes accessed | tf_op | source)
XLA Modules:
  0.0 111.5 jit_solution(8127654979142216595)
XLA Ops:
  1.9 6.1 %shard_map.217 = (bf16[256,512]{1,0:T(8,128)(2,1)}, bf16[256,512]{1,0:T(8,128)(2,1)}, bf16[16,2048]{1,0:T(8,128)(2,1)}, bf16[16,2048]{1,0:T(8,128)(2,1)}, bf16[2,16,512]{2,1,0:T(8,128)(2,1)}) custom-call(bf16[2048,512]{1,0:T(8,128)(2,1)} %own.1, bf16[2048,512]{1,0:T(8,128)(2,1)} %own.1, f32[4,2048]{1,0:T(4,128)} %enc_a.1, f32[4,2048]{1,0:T(4,128)} %proc_a.1, ...), custom_call_target="tpu_custom_call" | custom-call | tf_op jit(solution)/shard_map/pallas_call | solution.py:537
  8.0 7.8 %shard_map.218 = (bf16[256,512]{1,0:T(8,128)(2,1)}, bf16[256,512]{1,0:T(8,128)(2,1)}, f32[256,512]{1,0:T(8,128)}, bf16[2048,512]{1,0:T(8,128)(2,1)}, bf16[1024,512]{1,0:T(8,128)(2,1)}) custom-call(s32[16]{0:T(128)} %send_block.5, s32[16]{0:T(128)} %recv_block.5, s32[1]{0:T(128)S(6)} %copy.33.count, bf16[2048,512]{1,0:T(8,128)(2,1)} %own.1, ...), custom_call_target="tpu_custom_call" | custom-call | flops 4000000000 | bytes 10000000 | tf_op jit(solution)/shard_map/pallas_call | solution.py:559
  15.9 9.9 %shard_map.219 = (bf16[64,512]{1,0:T(8,128)(2,1)}, bf16[64,512]{1,0:T(8,128)(2,1)}) custom-call(bf16[256,512]{1,0:T(8,128)(2,1)} %get-tuple-element.31.up.down.enc_out, bf16[256,512]{1,0:T(8,128)(2,1)} %get-tuple-element.31.up.down.enc_out), custom_call_target="tpu_custom_call" | custom-call | tf_op jit(solution)/shard_map/pallas_call | solution.py:346
  25.8 8.3 %shard_map.220 = (bf16[256,512]{1,0:T(8,128)(2,1)}, f32[256,512]{1,0:T(8,128)}, bf16[64,512]{1,0:T(8,128)(2,1)}, bf16[64,512]{1,0:T(8,128)(2,1)}, bf16[16,32,2176]{2,1,0:T(8,128)(2,1)}) custom-call(s32[16]{0:T(128)} %send_block.4, s32[16]{0:T(128)} %recv_block.4, s32[1]{0:T(128)S(6)} %copy.34.count, bf16[256,512]{1,0:T(8,128)(2,1)} %get-tuple-element.31.up.down.enc_out, ...), custom_call_target="tpu_custom_call" | custom-call | flops 8000000000 | bytes 10000000 | tf_op jit(solution)/shard_map/pallas_call | solution.py:581
  34.1 71.1 %shard_map.221 = (bf16[256,512]{1,0:T(8,128)(2,1)}, bf16[2048,512]{1,0:T(8,128)(2,1)}, f32[32,2176]{1,0:T(8,128)}, f32[32,2176]{1,0:T(8,128)}) custom-call(s32[16]{0:T(128)} %send_block.5, s32[16]{0:T(128)} %recv_block.5, f32[256,512]{1,0:T(8,128)} %get-tuple-element.36.d_latent, bf16[64,512]{1,0:T(8,128)(2,1)} %get-tuple-element.37.rim_up, ...), custom_call_target="tpu_custom_call" | custom-call | tf_op jit(solution)/shard_map/pallas_call | solution.py:609
  105.2 0.0 copy-start
  105.2 1.2 %fusion = f32[2,32,2048]{2,1,0:T(8,128)S(1)} fusion(f32[1,32,2176]{2,1,0:T(8,128)} %bitcast.12, f32[1,32,2176]{2,1,0:T(8,128)} %bitcast.14), kind=kLoop, calls=%fused_computation.2 | loop fusion | flops 131072 | bytes 1081344 | tf_op jit(solution)/shard_map/stack | solution.py:642
  106.4 0.8 copy.30
  107.3 0.7 fusion.1
  108.0 0.7 slice_reduce_fusion
  108.7 0.1 slice_add_fusion
  108.8 0.7 copy.27
  109.5 0.0 copy-done
  109.5 0.0 copy-start.1
  109.5 1.3 %copy.35 = bf16[2048,512]{1,0:T(8,128)(2,1)} copy(bf16[2048,512]{1,0:T(8,128)(2,1)S(1)} %copy-done) | data formatting | bytes 4194304
  110.8 0.0 copy-done.1
  110.8 0.7 copy.36
Async XLA Ops:
  105.2 4.3 %copy-start = (bf16[2048,512]{1,0:T(8,128)(2,1)S(1)}, bf16[2048,512]{1,0:T(8,128)(2,1)}, u32[]{:S(2)}) copy-start(bf16[2048,512]{1,0:T(8,128)(2,1)} %get-tuple-element.67) | copy-start | bytes 6291460
  109.5 1.3 %copy-start.1 = (bf16[256,512]{1,0:T(8,128)(2,1)S(1)}, bf16[256,512]{1,0:T(8,128)(2,1)}, u32[]{:S(2)}) copy-start(bf16[256,512]{1,0:T(8,128)(2,1)} %get-tuple-element.68) | copy-start | bytes 786436

commit v3 on v2

--- a/solution.py
+++ b/solution.py
@@ -103,8 +103,6 @@
 
 def halving_order(parts, layer):
     order = list(range(parts.bit_length() - 1))
-    if layer == 0 and len(order) > 2:
-        order[1], order[2] = order[2], order[1]
     return order
 
 
@@ -125,11 +123,11 @@
         ].astype(bf16)
 
 
-def write_small(w_ref, layer, d_emb, d_gain):
+def write_small(w_ref, layer, column, d_emb, d_gain):
     width = d_emb.shape[1]
     pad = jnp.zeros((SMALL - 16 - 8, width), f32)
     block = jnp.concatenate([d_emb, jnp.broadcast_to(d_gain, (8, width)), pad], axis=0)
-    write_shards(w_ref, layer, 4 * width, block.T)
+    write_shards(w_ref, layer, column, block.T)
 
 
 def enc_forward_kernel(
@@ -244,7 +242,7 @@
     write_shards(w_out, 1, width, dot_ta(d_recv, latent))
     write_shards(w_out, 1, 2 * width, dot_ta(g, latent))
     write_shards(w_out, 1, 3 * width, dot_ta(g, agg))
-    write_small(w_out, 1, d_emb_acc[...], d_gain)
+    write_small(w_out, 1, 4 * width, d_emb_acc[...], d_gain)
 
 
 smem = pl.BlockSpec(memory_space=pltpu.SMEM)
@@ -371,17 +369,18 @@
     parts, send_block, recv_block, d_latent, rim_up, rim_down, latent, agg, mixed, slopes, tiles,
     w, gains, attr, send_slot, recv_slot, proc_w,
     mesh_grad, grid_grad, enc_out, proc_out,
-    back_lo, back_hi, grid_lo, grid_hi, from_prev, from_next, enc_w, d_rows, acc, d_emb_acc,
+    back_lo, back_hi, grid_lo, grid_hi, from_prev, from_next, enc_w, node_w, d_rows, acc, d_emb_acc,
     w0_acc, cot_ref, *scratch,
 ):
     rim_send, rim_recv, halo_send, halo_recv, send_sem, recv_sem = scratch[-6:]
     stages = parts.bit_length() - 1
-    landing = [scratch[0:stages], scratch[stages : 2 * stages]]
-    kept = [scratch[2 * stages : 3 * stages - 1], scratch[3 * stages - 1 : 4 * stages - 2]]
-    outs = [enc_out, proc_out]
-    current = [enc_w, proc_w]
-    copies = [None, None]
-    done = [0, 0]
+    span = 2 * stages - 1
+    landing = [scratch[k * span : k * span + stages] for k in range(3)]
+    kept = [scratch[k * span + stages : (k + 1) * span] for k in range(3)]
+    wide, side = 2 * latent.shape[1], 4 * latent.shape[1]
+    current = [enc_w, proc_w, node_w]
+    copies = [None] * 3
+    done = [0] * 3
     me = lax.axis_index("space")
 
     def bit_of(bit):
@@ -411,7 +410,14 @@
         source, arrived = current[layer], landing[layer][stage]
         done[layer] += 1
         if stage == stages - 1:
-            outs[layer][...] = source[mine].astype(f32) + arrived[0].astype(f32)
+            total = source[mine].astype(f32) + arrived[0].astype(f32)
+            if layer == 1:
+                proc_out[...] = total
+            elif layer == 2:
+                enc_out[:, wide:side] = total
+            else:
+                enc_out[:, 0:wide] = total[:, 0:wide]
+                enc_out[:, side:] = total[:, wide:]
             return
         target = kept[layer][stage]
 
@@ -446,8 +452,9 @@
     cot = cot_ref[...].astype(bf16).astype(f32)
     g, d_gain = tail_backward(mixed[...], cot, gains[0:1, :])
     d_agg = dot_tb(g, w[0, 3]).astype(bf16)
-    write_shards(enc_w, 0, 2 * width, dot_ta(g, latent[...]))
-    write_shards(enc_w, 0, 3 * width, dot_ta(g, agg[...]))
+    write_shards(node_w, 0, 0, dot_ta(g, latent[...]))
+    write_shards(node_w, 0, width, dot_ta(g, agg[...]))
+    start(2)
     for group in range(groups):
         tile = pl.ds(group * GB * BLK, GB * BLK)
         d_send, d_recv, d_emb = edges_backward(
@@ -459,13 +466,15 @@
         acc[...] += d_recv
         d_emb_acc[...] += d_emb
         w0_acc[...] += dot_ta(d_send, tiles[tile, :])
-        if group in (0, groups - 1):
+        if group == 0:
             advance(1)
+        if group == 1:
+            advance(2)
 
     d_recv = acc[...].astype(bf16)
     write_shards(enc_w, 0, 0, w0_acc[...])
     write_shards(enc_w, 0, width, dot_ta(d_recv, latent[...]))
-    write_small(enc_w, 0, d_emb_acc[...], d_gain)
+    write_small(enc_w, 0, 2 * width, d_emb_acc[...], d_gain)
     start(0)
 
     own = grid_grad.shape[0]
@@ -483,14 +492,17 @@
     grid_hi[...] = scattered(own // HG + 1)
     start_halo(parts, *halos)
     middle = own // HG // 2
+    advance(1)
     advance(0)
     lax.fori_loop(0, middle, own_chunk, 0)
+    advance(2)
     advance(1)
     lax.fori_loop(middle, own // HG, own_chunk, 0)
     mesh_grad[...] = (cot + dot_tb(g, w[0, 2]) + dot_tb(d_recv, w[0, 1])).astype(bf16)
     for _ in range(stages):
+        advance(1)
+        advance(2)
         advance(0)
-        advance(1)
     finish_halo(parts, *halos)
     grid_grad[0:HG, :] += from_prev[...]
     grid_grad[own - HG :, :] += from_next[...]
@@ -605,7 +617,10 @@
     stages = parts.bit_length() - 1
     columns = 4 * width + SMALL
     shard = width // parts
-    landing = [pltpu.VMEM((parts >> (k + 1), shard, columns), bf16) for k in range(stages)]
+    streams = []
+    for wide in (2 * width + SMALL, columns, 2 * width):
+        landing = [pltpu.VMEM((parts >> (k + 1), shard, wide), bf16) for k in range(stages)]
+        streams += landing + landing[:-1]
     mesh_grad, grid_grad, enc_sum, proc_sum = pl.pallas_call(
         functools.partial(enc_backward_kernel, parts),
         grid=(1,),
@@ -620,17 +635,17 @@
         scratch_shapes=[pltpu.VMEM((HM, width), bf16)] * 2
         + [pltpu.VMEM((HG, width), bf16)] * 4
         + [
-            pltpu.VMEM((parts, shard, columns), bf16),
+            pltpu.VMEM((parts, shard, 2 * width + SMALL), bf16),
+            pltpu.VMEM((parts, shard, 2 * width), bf16),
             pltpu.VMEM((blocks * BLK, width), bf16),
             pltpu.VMEM((rows, width), f32),
             pltpu.VMEM((16, width), f32),
             pltpu.VMEM((width, width), f32),
             pltpu.VMEM((rows, width), f32),
         ]
-        + landing * 2
-        + landing[:-1] * 2
+        + streams
         + [pltpu.SemaphoreType.DMA((2,))] * 4
-        + [pltpu.SemaphoreType.DMA((2, stages))] * 2,
+        + [pltpu.SemaphoreType.DMA((3, stages))] * 2,
         compiler_params=pltpu.CompilerParams(
             collective_id=2, has_side_effects=True, vmem_limit_bytes=VMEM_LIMIT
         ),

time: 112 us -> 101 us (0.902)
  Pallas kernels: 103 us -> 92.5 us
    pallas_call x1, Pallas kernels: 71.1 us -> 56.3 us  [per_device(): pl.pallas_call(functools.partial(enc_backward_kernel, parts), grid=(1,),...]
    pallas_call x1, Pallas kernels: 9.91 us -> 12.1 us  [exchange(): pl.pallas_call(functools.partial(exchange_kernel, parts), grid=(1,), in_s...]
    pallas_call x1, Pallas kernels: 8.3 us -> 10.1 us  [per_device(): call(proc_kernel, [smem] * 3 + [vmem] * 4 + [layer_spec(1, matrices.shape...]
where the time goes in v3:
time: 101 us
  Pallas kernels  92.5 us (92%)
  local copies, waits for them, and re-layouts  4.27 us (4%)
  other arithmetic  2.03 us (2%)
  between operations  1.98 us (2%)
    pallas_call x1, Pallas kernels, per_device(): pl.pallas_call(functools.partial(enc_backward_kernel, parts), grid=(1,),...  56.3 us
    pallas_call x1, Pallas kernels, exchange(): pl.pallas_call(functools.partial(exchange_kernel, parts), grid=(1,), in_s...  12.1 us
    pallas_call x1, Pallas kernels, per_device(): call(proc_kernel, [smem] * 3 + [vmem] * 4 + [layer_spec(1, matrices.shape...  10.1 us
    pallas_call x1, Pallas kernels, per_device(): call(enc_forward_kernel, [smem] * 3 + [hbm] * 3 + [vmem, layer_spec(0, ma...  7.84 us
    pallas_call x1, Pallas kernels, per_device(): pl.pallas_call(functools.partial(first_exchange_kernel, parts), grid=(1,)...  6.08 us
    unnamed x7, local copies, waits for them, and re-layouts  2.71 us

profile of v3, /device:TPU:0, one launch (start us, length us, event | category | flops | bytes accessed | tf_op | source)
XLA Modules:
  0.0 100.7 jit_solution(6768678174762204314)
XLA Ops:
  1.9 6.1 %shard_map.217 = (bf16[256,512]{1,0:T(8,128)(2,1)}, bf16[256,512]{1,0:T(8,128)(2,1)}, bf16[16,2048]{1,0:T(8,128)(2,1)}, bf16[16,2048]{1,0:T(8,128)(2,1)}, bf16[2,16,512]{2,1,0:T(8,128)(2,1)}) custom-call(bf16[2048,512]{1,0:T(8,128)(2,1)} %own.1, bf16[2048,512]{1,0:T(8,128)(2,1)} %own.1, f32[4,2048]{1,0:T(4,128)} %enc_a.1, f32[4,2048]{1,0:T(4,128)} %proc_a.1, ...), custom_call_target="tpu_custom_call" | custom-call | tf_op jit(solution)/shard_map/pallas_call | solution.py:549
  8.0 7.8 %shard_map.218 = (bf16[256,512]{1,0:T(8,128)(2,1)}, bf16[256,512]{1,0:T(8,128)(2,1)}, f32[256,512]{1,0:T(8,128)}, bf16[2048,512]{1,0:T(8,128)(2,1)}, bf16[1024,512]{1,0:T(8,128)(2,1)}) custom-call(s32[16]{0:T(128)} %send_block.5, s32[16]{0:T(128)} %recv_block.5, s32[1]{0:T(128)S(6)} %copy.33.count, bf16[2048,512]{1,0:T(8,128)(2,1)} %own.1, ...), custom_call_target="tpu_custom_call" | custom-call | flops 4000000000 | bytes 10000000 | tf_op jit(solution)/shard_map/pallas_call | solution.py:571
  15.9 12.1 %shard_map.219 = (bf16[64,512]{1,0:T(8,128)(2,1)}, bf16[64,512]{1,0:T(8,128)(2,1)}) custom-call(bf16[256,512]{1,0:T(8,128)(2,1)} %get-tuple-element.31.up.down.enc_out, bf16[256,512]{1,0:T(8,128)(2,1)} %get-tuple-element.31.up.down.enc_out), custom_call_target="tpu_custom_call" | custom-call | tf_op jit(solution)/shard_map/pallas_call | solution.py:344
  28.0 10.1 %shard_map.220 = (bf16[256,512]{1,0:T(8,128)(2,1)}, f32[256,512]{1,0:T(8,128)}, bf16[64,512]{1,0:T(8,128)(2,1)}, bf16[64,512]{1,0:T(8,128)(2,1)}, bf16[16,32,2176]{2,1,0:T(8,128)(2,1)}) custom-call(s32[16]{0:T(128)} %send_block.4, s32[16]{0:T(128)} %recv_block.4, s32[1]{0:T(128)S(6)} %copy.34.count, bf16[256,512]{1,0:T(8,128)(2,1)} %get-tuple-element.31.up.down.enc_out, ...), custom_call_target="tpu_custom_call" | custom-call | flops 8000000000 | bytes 10000000 | tf_op jit(solution)/shard_map/pallas_call | solution.py:593
  38.1 56.3 %shard_map.221 = (bf16[256,512]{1,0:T(8,128)(2,1)}, bf16[2048,512]{1,0:T(8,128)(2,1)}, f32[32,2176]{1,0:T(8,128)}, f32[32,2176]{1,0:T(8,128)}) custom-call(s32[16]{0:T(128)} %send_block.5, s32[16]{0:T(128)} %recv_block.5, f32[256,512]{1,0:T(8,128)} %get-tuple-element.36.d_latent, bf16[64,512]{1,0:T(8,128)(2,1)} %get-tuple-element.37.rim_up, ...), custom_call_target="tpu_custom_call" | custom-call | tf_op jit(solution)/shard_map/pallas_call | solution.py:624
  94.4 0.0 copy-start
  94.4 1.2 %fusion = f32[2,32,2048]{2,1,0:T(8,128)S(1)} fusion(f32[1,32,2176]{2,1,0:T(8,128)} %bitcast.12, f32[1,32,2176]{2,1,0:T(8,128)} %bitcast.14), kind=kLoop, calls=%fused_computation.2 | loop fusion | flops 131072 | bytes 1081344 | tf_op jit(solution)/shard_map/stack | solution.py:657
  95.6 0.8 copy.30
  96.5 0.7 fusion.1
  97.2 0.7 slice_reduce_fusion
  98.0 0.1 slice_add_fusion
  98.0 0.7 copy.27
  98.7 0.0 copy-done
  98.7 0.0 copy-start.1
  98.7 1.3 %copy.35 = bf16[2048,512]{1,0:T(8,128)(2,1)} copy(bf16[2048,512]{1,0:T(8,128)(2,1)S(1)} %copy-done) | data formatting | bytes 4194304
  100.0 0.0 copy-done.1
  100.0 0.7 copy.36
Async XLA Ops:
  94.4 4.3 %copy-start = (bf16[2048,512]{1,0:T(8,128)(2,1)S(1)}, bf16[2048,512]{1,0:T(8,128)(2,1)}, u32[]{:S(2)}) copy-start(bf16[2048,512]{1,0:T(8,128)(2,1)} %get-tuple-element.67) | copy-start | bytes 6291460
  98.7 1.3 %copy-start.1 = (bf16[256,512]{1,0:T(8,128)(2,1)S(1)}, bf16[256,512]{1,0:T(8,128)(2,1)}, u32[]{:S(2)}) copy-start(bf16[256,512]{1,0:T(8,128)(2,1)} %get-tuple-element.68) | copy-start | bytes 786436
